TPU v7x, 32 devices: a whole 2x2x4 slice. The times are simulated.
32 devices in a mesh: dom: 16 (over z, y, x), cls: 2 (over core).
Axes of the slice: x: 2, y: 2, z: 4, core: 2. Of those that a mesh axis runs over, the one named last changes fastest.
Arguments:
- particles: bfloat16 [2048, 4608], P('dom'), may hold values from -80 to 80
- references: bfloat16 [32, 4608], P(('cls', 'dom')), may hold values from -0.77 to 0.77
- log_prior: float32 [32], P('cls'), may hold values from -3 to 3
- noise_var: float32 [32], replicated, may hold values from 0.5 to 2
- offsets: int32 [2048, 2], P('dom'), may hold values from -4 to 4
- groups: int32 [2048], P('dom'), may hold values from 0 to 15
Outputs:
- class_data: float32 [32, 4608], P(('cls', 'dom'))
- class_weight: float32 [32, 32], P(('cls', 'dom'))
- log_evidence: float32 [2048], P('dom')
All inputs are finite; a program needn't handle non-finite values.
Results may differ from a plain program's by a relative error of at most 0.011.
Values may be sent and summed in bfloat16 or wider, within the bound.
No kernel may reach another device: no remote copies, remote signals or barrier semaphores. Data moves between devices by JAX's collectives and lax.ppermute only.
A program may use at most 64 MiB of HBM per device.

v0:
```python
import math

import jax
import jax.numpy as jnp
from jax import lax
from jax.sharding import PartitionSpec as P

BOX = 64
CYCLES = 32
ROT = 36
ANGLES = 72
SAMPLES = 4608


def prepare(observed_raw, offsets, groups, noise_var):
    row_count = observed_raw.shape[0]
    observed = observed_raw.astype(jnp.float32).reshape(row_count, ANGLES, 2, CYCLES)
    radius = jnp.arange(CYCLES, dtype=jnp.float32) + 1.0
    angle_rad = 2.0 * math.pi * jnp.arange(ANGLES, dtype=jnp.float32) / ANGLES
    shift_x = offsets[:, 0].astype(jnp.float32)
    shift_y = offsets[:, 1].astype(jnp.float32)
    phase_angle = (
        -2.0
        * math.pi
        / BOX
        * radius[None, None, :]
        * (
            shift_x[:, None, None] * jnp.cos(angle_rad)[None, :, None]
            + shift_y[:, None, None] * jnp.sin(angle_rad)[None, :, None]
        )
    )
    frequency = radius / (1.5 * BOX)
    defocus = 10000.0 + 1500.0 * groups.astype(jnp.float32)
    chi_value = math.pi * 0.0197 * defocus[:, None] * (frequency * frequency)[None, :]
    ctf_rows = (
        -(0.995 * jnp.sin(chi_value) + 0.1 * jnp.cos(chi_value))
        * jnp.exp(-10.0 * frequency * frequency)[None, :]
    )
    cycle_scale = ctf_rows / noise_var[None, :]
    cosine = jnp.cos(phase_angle)
    sine_part = jnp.sin(phase_angle)
    real_in = observed[:, :, 0, :]
    imag_in = observed[:, :, 1, :]
    real_out = cycle_scale[:, None, :] * (real_in * cosine + imag_in * sine_part)
    imag_out = cycle_scale[:, None, :] * (imag_in * cosine - real_in * sine_part)
    adjusted = (
        jnp.stack([real_out, imag_out], axis=2).reshape(row_count, SAMPLES).astype(jnp.bfloat16)
    )
    ctf_power = ctf_rows * ctf_rows / noise_var[None, :]
    return (adjusted, ctf_power)


def per_device(particles, references, log_prior, noise_var, offsets, groups):
    ref_block = lax.all_gather(references, "dom", axis=0, tiled=True)
    adjusted, ctf_power = prepare(particles, offsets, groups, noise_var)
    row_count = adjusted.shape[0]
    sample_len = adjusted.shape[1]
    cycle_count = noise_var.shape[0]
    class_count = ref_block.shape[0]
    shift_unit = sample_len // ROT
    group_size = 3
    group_count = ROT // group_size
    doubled = jnp.concatenate([adjusted, adjusted], axis=1)

    def rotate_group(group_idx):
        pieces = [
            lax.dynamic_slice_in_dim(
                doubled, (group_idx * group_size + member) * shift_unit, sample_len, 1
            )
            for member in range(group_size)
        ]
        return jnp.stack(pieces, axis=0)

    def score_group(group_idx, running):
        rotated = rotate_group(group_idx)
        block_scores = jnp.einsum(
            "cn,rpn->rcp", ref_block, rotated, preferred_element_type=jnp.float32
        )
        return lax.dynamic_update_slice_in_dim(running, block_scores, group_idx * group_size, 0)

    cross_terms = lax.fori_loop(
        0, group_count, score_group, jnp.zeros((ROT, class_count, row_count), jnp.float32)
    )
    ref_float = ref_block.astype(jnp.float32).reshape(class_count, -1, cycle_count)
    ref_power = jnp.sum(ref_float * ref_float, axis=1)
    energy = 0.5 * jnp.dot(ref_power, ctf_power.T, precision=lax.Precision.HIGHEST)
    scores = cross_terms - energy[None, :, :] + log_prior[None, :, None]
    best_local = jnp.max(scores, axis=(0, 1))
    best = lax.pmax(best_local, "cls")
    total_sum = lax.psum(jnp.sum(jnp.exp(scores - best[None, None, :]), axis=(0, 1)), "cls")
    log_evidence = best + jnp.log(total_sum)
    posterior = jnp.exp(scores - log_evidence[None, None, :])
    posterior_bf = posterior.astype(jnp.bfloat16)

    def accumulate(group_idx, running):
        rotated = rotate_group(group_idx)
        weights = lax.dynamic_slice_in_dim(posterior_bf, group_idx * group_size, group_size, 0)
        return running + jnp.einsum(
            "rcp,rpn->cn", weights, rotated, preferred_element_type=jnp.float32
        )

    class_data = lax.fori_loop(
        0, group_count, accumulate, jnp.zeros((class_count, sample_len), jnp.float32)
    )
    class_weight = jnp.dot(jnp.sum(posterior, axis=0), ctf_power, precision=lax.Precision.HIGHEST)
    data_total, weight_total = lax.psum((class_data, class_weight), "dom")
    owned_rows = class_count // lax.axis_size("dom")
    first_row = lax.axis_index("dom") * owned_rows
    data_owned = lax.dynamic_slice_in_dim(data_total, first_row, owned_rows, 0)
    weight_owned = lax.dynamic_slice_in_dim(weight_total, first_row, owned_rows, 0)
    return (data_owned, weight_owned, log_evidence)


def solution(mesh):
    return jax.shard_map(
        per_device,
        mesh=mesh,
        in_specs=(P("dom", None), P(("cls", "dom"), None), P("cls"), P(), P("dom", None), P("dom")),
        out_specs=(P(("cls", "dom"), None), P(("cls", "dom"), None), P("dom")),
        check_vma=False,
    )
```

profile of v0, /device:TPU:0, one launch (start us, length us, event | category | flops | bytes accessed | tf_op | source)
XLA Modules:
  0.0 312.3 jit_solution(8978844706792634432)
XLA Ops:
  8.7 1.7 copy.15
  11.3 5.0 %fusion.29 = (bf16[128,72,1,32]{0,3,2,1:T(8,128)(2,1)S(1)}, bf16[128,72,1,32]{0,3,2,1:T(8,128)(2,1)S(1)}) fusion(f32[128,72,2,32]{0,3,2,1:T(8,128)S(1)} %convert.9, f32[128,72]{0,1:T(8,128)S(1)} %multiply_add_fusion, f32[32]{0:T(128)S(1)} %fusion.45, f32[128,32]{0,1:T(8,128)S(1)} %fusion.41), kind=kLoop, calls=%fused_computation.35 | loop fusion | flops 3244032 | bytes 3592320 | tf_op jit(solution)/shard_map/convert.1
  16.5 9.3 %pad_maximum_fusion = bf16[128,9216]{0,1:T(8,128)(2,1)} fusion(bf16[128,4608]{0,1:T(8,128)(2,1)S(1)} %bitcast.46), kind=kLoop, calls=%fused_computation.26 | loop fusion | flops 4718592 | bytes 3538944 | tf_op jit(solution)/shard_map/concatenate | solution.py:63
  25.8 2.8 copy.16
  28.6 43.9 %all-gather = bf16[16,1,4608]{2,1,0:T(2,128)(2,1)S(1)} all-gather(bf16[1,1,4608]{2,1,0:T(2,128)(2,1)S(1)} %bitcast.48), channel_id=1, replica_groups=mesh['dom'=16,'cls'=2] {'dom'}, dimensions={0}, use_global_device_ids=true | all-gather | bytes 156672 | tf_op jit(solution)/shard_map/all_gather | solution.py:54
  74.1 59.2 %while.31 = (s32[]{:T(128)}, f32[36,16,128]{2,1,0:T(8,128)}, bf16[128,9216]{1,0:T(8,128)(2,1)S(1)}, bf16[16,4608]{1,0:T(8,128)(2,1)}, s32[]{:T(128)}, /*index=5*...) while((s32[]{:T(128)}, f32[36,16,128]{2,1,0:T(8,128)}, ...), condition=%wide.region_1.0_spmd, body=%wide.region_0.0_spmd.sunk | while | flops 60162068 | bytes 10789205 | solution.py:81
  74.1 1.6 dynamic-slice_bitcast_fusion.8
  75.8 3.3 %fusion.62 = f32[36,16,128]{2,1,0:T(8,128)} fusion(f32[36,16,128]{2,1,0:T(8,128)} %get-tuple-element.373, s32[]{:T(128)S(6)} %select_n.97, bf16[1,128,4608]{2,1,0:T(8,128)(2,1)} %get-tuple-element.350, bf16[1,128,4608]{2,1,0:T(8,128)(2,1)} %get-tuple-element.351, bf16[1,128,4608]{2,1,0:T(8,128)(2,1)S(1)} %get-tuple-element.352, ...), kind=kOutput, calls=%fused_computation.10.clone.1 | convolution fusion | flops 60162048 | bytes 3710980 | tf_op jit(solution)/shard_map/while/body/eval_jaxpr/cn,rpn->rcp/dot_general | solution.py:76
  79.1 1.6 dynamic-slice_bitcast_fusion.8
  80.7 3.3 %fusion.62 = f32[36,16,128]{2,1,0:T(8,128)} fusion(f32[36,16,128]{2,1,0:T(8,128)} %get-tuple-element.373, s32[]{:T(128)S(6)} %select_n.97, bf16[1,128,4608]{2,1,0:T(8,128)(2,1)} %get-tuple-element.350, bf16[1,128,4608]{2,1,0:T(8,128)(2,1)} %get-tuple-element.351, bf16[1,128,4608]{2,1,0:T(8,128)(2,1)S(1)} %get-tuple-element.352, ...), kind=kOutput, calls=%fused_computation.10.clone.1 | convolution fusion | flops 60162048 | bytes 3710980 | tf_op jit(solution)/shard_map/while/body/eval_jaxpr/cn,rpn->rcp/dot_general | solution.py:76
  84.0 1.6 dynamic-slice_bitcast_fusion.8
  85.6 3.3 %fusion.62 = f32[36,16,128]{2,1,0:T(8,128)} fusion(f32[36,16,128]{2,1,0:T(8,128)} %get-tuple-element.373, s32[]{:T(128)S(6)} %select_n.97, bf16[1,128,4608]{2,1,0:T(8,128)(2,1)} %get-tuple-element.350, bf16[1,128,4608]{2,1,0:T(8,128)(2,1)} %get-tuple-element.351, bf16[1,128,4608]{2,1,0:T(8,128)(2,1)S(1)} %get-tuple-element.352, ...), kind=kOutput, calls=%fused_computation.10.clone.1 | convolution fusion | flops 60162048 | bytes 3710980 | tf_op jit(solution)/shard_map/while/body/eval_jaxpr/cn,rpn->rcp/dot_general | solution.py:76
  88.9 1.6 dynamic-slice_bitcast_fusion.8
  90.6 3.3 %fusion.62 = f32[36,16,128]{2,1,0:T(8,128)} fusion(f32[36,16,128]{2,1,0:T(8,128)} %get-tuple-element.373, s32[]{:T(128)S(6)} %select_n.97, bf16[1,128,4608]{2,1,0:T(8,128)(2,1)} %get-tuple-element.350, bf16[1,128,4608]{2,1,0:T(8,128)(2,1)} %get-tuple-element.351, bf16[1,128,4608]{2,1,0:T(8,128)(2,1)S(1)} %get-tuple-element.352, ...), kind=kOutput, calls=%fused_computation.10.clone.1 | convolution fusion | flops 60162048 | bytes 3710980 | tf_op jit(solution)/shard_map/while/body/eval_jaxpr/cn,rpn->rcp/dot_general | solution.py:76
  93.9 1.6 dynamic-slice_bitcast_fusion.8
  95.5 3.3 %fusion.62 = f32[36,16,128]{2,1,0:T(8,128)} fusion(f32[36,16,128]{2,1,0:T(8,128)} %get-tuple-element.373, s32[]{:T(128)S(6)} %select_n.97, bf16[1,128,4608]{2,1,0:T(8,128)(2,1)} %get-tuple-element.350, bf16[1,128,4608]{2,1,0:T(8,128)(2,1)} %get-tuple-element.351, bf16[1,128,4608]{2,1,0:T(8,128)(2,1)S(1)} %get-tuple-element.352, ...), kind=kOutput, calls=%fused_computation.10.clone.1 | convolution fusion | flops 60162048 | bytes 3710980 | tf_op jit(solution)/shard_map/while/body/eval_jaxpr/cn,rpn->rcp/dot_general | solution.py:76
  98.8 1.6 dynamic-slice_bitcast_fusion.8
  100.4 3.3 %fusion.62 = f32[36,16,128]{2,1,0:T(8,128)} fusion(f32[36,16,128]{2,1,0:T(8,128)} %get-tuple-element.373, s32[]{:T(128)S(6)} %select_n.97, bf16[1,128,4608]{2,1,0:T(8,128)(2,1)} %get-tuple-element.350, bf16[1,128,4608]{2,1,0:T(8,128)(2,1)} %get-tuple-element.351, bf16[1,128,4608]{2,1,0:T(8,128)(2,1)S(1)} %get-tuple-element.352, ...), kind=kOutput, calls=%fused_computation.10.clone.1 | convolution fusion | flops 60162048 | bytes 3710980 | tf_op jit(solution)/shard_map/while/body/eval_jaxpr/cn,rpn->rcp/dot_general | solution.py:76
  103.7 1.6 dynamic-slice_bitcast_fusion.8
  105.4 3.3 %fusion.62 = f32[36,16,128]{2,1,0:T(8,128)} fusion(f32[36,16,128]{2,1,0:T(8,128)} %get-tuple-element.373, s32[]{:T(128)S(6)} %select_n.97, bf16[1,128,4608]{2,1,0:T(8,128)(2,1)} %get-tuple-element.350, bf16[1,128,4608]{2,1,0:T(8,128)(2,1)} %get-tuple-element.351, bf16[1,128,4608]{2,1,0:T(8,128)(2,1)S(1)} %get-tuple-element.352, ...), kind=kOutput, calls=%fused_computation.10.clone.1 | convolution fusion | flops 60162048 | bytes 3710980 | tf_op jit(solution)/shard_map/while/body/eval_jaxpr/cn,rpn->rcp/dot_general | solution.py:76
  108.7 1.6 dynamic-slice_bitcast_fusion.8
  110.3 3.3 %fusion.62 = f32[36,16,128]{2,1,0:T(8,128)} fusion(f32[36,16,128]{2,1,0:T(8,128)} %get-tuple-element.373, s32[]{:T(128)S(6)} %select_n.97, bf16[1,128,4608]{2,1,0:T(8,128)(2,1)} %get-tuple-element.350, bf16[1,128,4608]{2,1,0:T(8,128)(2,1)} %get-tuple-element.351, bf16[1,128,4608]{2,1,0:T(8,128)(2,1)S(1)} %get-tuple-element.352, ...), kind=kOutput, calls=%fused_computation.10.clone.1 | convolution fusion | flops 60162048 | bytes 3710980 | tf_op jit(solution)/shard_map/while/body/eval_jaxpr/cn,rpn->rcp/dot_general | solution.py:76
  113.6 1.6 dynamic-slice_bitcast_fusion.8
  115.3 3.3 %fusion.62 = f32[36,16,128]{2,1,0:T(8,128)} fusion(f32[36,16,128]{2,1,0:T(8,128)} %get-tuple-element.373, s32[]{:T(128)S(6)} %select_n.97, bf16[1,128,4608]{2,1,0:T(8,128)(2,1)} %get-tuple-element.350, bf16[1,128,4608]{2,1,0:T(8,128)(2,1)} %get-tuple-element.351, bf16[1,128,4608]{2,1,0:T(8,128)(2,1)S(1)} %get-tuple-element.352, ...), kind=kOutput, calls=%fused_computation.10.clone.1 | convolution fusion | flops 60162048 | bytes 3710980 | tf_op jit(solution)/shard_map/while/body/eval_jaxpr/cn,rpn->rcp/dot_general | solution.py:76
  118.5 1.6 dynamic-slice_bitcast_fusion.8
  120.2 3.3 %fusion.62 = f32[36,16,128]{2,1,0:T(8,128)} fusion(f32[36,16,128]{2,1,0:T(8,128)} %get-tuple-element.373, s32[]{:T(128)S(6)} %select_n.97, bf16[1,128,4608]{2,1,0:T(8,128)(2,1)} %get-tuple-element.350, bf16[1,128,4608]{2,1,0:T(8,128)(2,1)} %get-tuple-element.351, bf16[1,128,4608]{2,1,0:T(8,128)(2,1)S(1)} %get-tuple-element.352, ...), kind=kOutput, calls=%fused_computation.10.clone.1 | convolution fusion | flops 60162048 | bytes 3710980 | tf_op jit(solution)/shard_map/while/body/eval_jaxpr/cn,rpn->rcp/dot_general | solution.py:76
  123.5 1.6 dynamic-slice_bitcast_fusion.8
  125.1 3.3 %fusion.62 = f32[36,16,128]{2,1,0:T(8,128)} fusion(f32[36,16,128]{2,1,0:T(8,128)} %get-tuple-element.373, s32[]{:T(128)S(6)} %select_n.97, bf16[1,128,4608]{2,1,0:T(8,128)(2,1)} %get-tuple-element.350, bf16[1,128,4608]{2,1,0:T(8,128)(2,1)} %get-tuple-element.351, bf16[1,128,4608]{2,1,0:T(8,128)(2,1)S(1)} %get-tuple-element.352, ...), kind=kOutput, calls=%fused_computation.10.clone.1 | convolution fusion | flops 60162048 | bytes 3710980 | tf_op jit(solution)/shard_map/while/body/eval_jaxpr/cn,rpn->rcp/dot_general | solution.py:76
  128.4 1.6 dynamic-slice_bitcast_fusion.8
  130.1 3.3 %fusion.62 = f32[36,16,128]{2,1,0:T(8,128)} fusion(f32[36,16,128]{2,1,0:T(8,128)} %get-tuple-element.373, s32[]{:T(128)S(6)} %select_n.97, bf16[1,128,4608]{2,1,0:T(8,128)(2,1)} %get-tuple-element.350, bf16[1,128,4608]{2,1,0:T(8,128)(2,1)} %get-tuple-element.351, bf16[1,128,4608]{2,1,0:T(8,128)(2,1)S(1)} %get-tuple-element.352, ...), kind=kOutput, calls=%fused_computation.10.clone.1 | convolution fusion | flops 60162048 | bytes 3710980 | tf_op jit(solution)/shard_map/while/body/eval_jaxpr/cn,rpn->rcp/dot_general | solution.py:76
  133.4 1.3 mul.328
  135.7 1.1 fusion.35
  136.8 2.5 pmax.7
  139.3 1.1 exponential_reduce_fusion
  140.4 2.5 psum.21
  142.9 1.8 fusion.33
  144.7 55.8 %while.32 = (s32[]{:T(128)}, f32[16,4608]{1,0:T(8,128)}, bf16[36,16,128]{2,1,0:T(8,128)(2,1)}, bf16[128,9216]{1,0:T(8,128)(2,1)S(1)}, s32[]{:T(128)}, /*index=5*...) while((s32[]{:T(128)}, f32[16,4608]{1,0:T(8,128)}, ...), condition=%wide.region_8.0_spmd.clone, body=%wide.region_7.0_spmd.clone.sunk | while | flops 60309524 | bytes 11219295 | solution.py:102
  144.7 1.6 dynamic-slice_bitcast_fusion.9
  146.3 3.0 fusion.65
  149.3 1.6 dynamic-slice_bitcast_fusion.9
  150.9 3.0 fusion.65
  153.9 1.6 dynamic-slice_bitcast_fusion.9
  155.6 3.0 fusion.65
  158.6 1.6 dynamic-slice_bitcast_fusion.9
  160.2 3.0 fusion.65
  163.2 1.6 dynamic-slice_bitcast_fusion.9
  164.9 3.0 fusion.65
  167.9 1.6 dynamic-slice_bitcast_fusion.9
  169.5 3.0 fusion.65
  172.5 1.6 dynamic-slice_bitcast_fusion.9
  174.2 3.0 fusion.65
  177.2 1.6 dynamic-slice_bitcast_fusion.9
  178.8 3.0 fusion.65
  181.8 1.6 dynamic-slice_bitcast_fusion.9
  183.5 3.0 fusion.65
  186.5 1.6 dynamic-slice_bitcast_fusion.9
  188.1 3.0 fusion.65
  191.1 1.6 dynamic-slice_bitcast_fusion.9
  192.8 3.0 fusion.65
  195.8 1.6 dynamic-slice_bitcast_fusion.9
  197.4 3.0 fusion.65
  201.4 37.1 %psum.23 = f32[16,32]{1,0:T(8,128)S(1)} all-reduce(f32[16,32]{1,0:T(8,128)S(1)} %fusion.42), channel_id=1, replica_groups=mesh['dom'=16,'cls'=2] {'dom'}, use_global_device_ids=true, to_apply=%region_11.0 | all-reduce | flops 512 | bytes 4096 | tf_op jit(solution)/shard_map/psum | solution.py:106
  239.1 64.8 %all-reduce.2.cloned.1.call-done = f32[16,4608]{1,0:T(8,128)} async-done(((f32[16,4608]{1,0:T(8,128)}), f32[16,4608]{1,0:T(8,128)}) %all-reduce.2.cloned.1.call-update) | async-done | bytes 294928 | tf_op jit(solution)/shard_map/psum | solution.py:106
  303.9 1.5 constant_dynamic-slice_fusion.1
  (35 shorter events, 6.6 us)
Async XLA Ops:
  7.2 296.7 %all-reduce.2.cloned.1.call-start = ((), (), s32[]{:S(2)}) async-start(), calls=%async_computation | async-start | bytes 589824 | tf_op jit(solution)/shard_map/psum | solution.py:106
  7.2 3.6 %copy-start.5 = (f32[32]{0:T(128)}, f32[32]{0:T(128)S(1)}, u32[]{:S(2)}) copy-start(f32[32]{0:T(128)S(1)} %get-tuple-element.296) | copy-start | bytes 388
  7.2 3.6 %copy-start.6 = (f32[32]{0:T(128)}, f32[32]{0:T(128)S(1)}, u32[]{:S(2)}) copy-start(f32[32]{0:T(128)S(1)} %get-tuple-element.297) | copy-start | bytes 388
  8.0 2.8 copy-start.7
  10.4 0.7 copy-start.3
  25.8 2.9 copy-start
  133.4 2.4 copy-start.1
  142.9 1.8 copy-start.2
  144.7 55.8 %copy-start.4 = (f32[32]{0:T(128)S(1)}, f32[32]{0:T(128)}, u32[]{:S(2)}) copy-start(f32[32]{0:T(128)} %param.13) | copy-start | bytes 388
Sparse Core Ops, SparseCore 0:
  200.6 103.2 all-reduce.1
where the time goes:
time: 314 us; the launch traced here: 312 us
  blocking collectives  86 us (27%)
  matrix products  77.4 us (25%)
  waiting for transfers between devices  64.8 us (21%)
  local copies, waits for them, and re-layouts  48.3 us (15%)
  other arithmetic  21.4 us (7%)
  between operations  14.2 us (5%)
    psum x1, waiting for transfers between devices, per_device(): data_total, weight_total = lax.psum((class_data, class_weight), 'dom')  64.8 us
    all_gather x1, blocking collectives, per_device(): ref_block = lax.all_gather(references, 'dom', axis=0, tiled=True)  43.9 us
    dot_general x12, matrix products, score_group(): jnp.einsum('cn,rpn->rcp', ref_block, rotated, preferred_element_type=jnp....  39.5 us
    another operation x24, local copies, waits for them, and re-layouts, rotate_group(): return jnp.stack(pieces, axis=0)  39.4 us
    psum x1, blocking collectives, per_device(): data_total, weight_total = lax.psum((class_data, class_weight), 'dom')  37.1 us
    dot_general x12, matrix products, accumulate(): jnp.einsum('rcp,rpn->cn', weights, rotated, preferred_element_type=jnp.fl...  36 us
    concatenate x1, other arithmetic, per_device(): doubled = jnp.concatenate([adjusted, adjusted], axis=1)  9.29 us
  transfers between devices with their start and end apart: 1, of which 1 were waited for; matrix products, arithmetic and copies ran while one was open for 0% of the time, Pallas kernels for 0%

commit v1 on v0

v1 whole, which is shorter than its diff:
```python
import functools
import math

import jax
import jax.numpy as jnp
import numpy as np
from jax import lax
from jax.experimental import pallas as pl
from jax.experimental.pallas import tpu as pltpu
from jax.sharding import PartitionSpec as P

BOX = 64
CYCLES = 32
ROT = 36
ANGLES = 72
LANES = 128
HALF = ROT // 2
CHUNK = 40
F32 = jnp.float32
BF16 = jnp.bfloat16
HIGHEST = lax.Precision.HIGHEST
VMEM_LIMIT = 24 * 1024 * 1024


def trig_polynomials():
    nodes = 0.125 + 0.125 * np.cos(np.pi * (np.arange(400) + 0.5) / 400)
    root = np.sqrt(nodes)
    fits = []
    for values, degree in ((np.cos(2 * np.pi * root), 7), (np.sin(2 * np.pi * root) / root, 7)):
        fit = np.polynomial.Chebyshev.fit(nodes, values, degree, domain=[0, 0.25])
        fits.append([float(c) for c in fit.convert(kind=np.polynomial.Polynomial).coef])
    return fits


COS_COEF, SIN_COEF = trig_polynomials()


def horner(coef, x):
    total = coef[-1] * x + coef[-2]
    for c in coef[-3::-1]:
        total = total * x + c
    return total


def turn_trig(turns):
    r = turns - jnp.floor(turns + 0.5)
    square = r * r
    return horner(COS_COEF, square), horner(SIN_COEF, square) * r


def lane_tables():
    lane = np.arange(LANES)
    cycle = lane % CYCLES
    rows = []
    for component in (np.cos, np.sin):
        for t in range(HALF):
            theta = 2.0 * np.pi * (2 * t + lane // 64) / ANGLES
            rows.append((cycle + 1.0) * component(theta) / BOX)
    square = ((cycle + 1.0) / (1.5 * BOX)) ** 2
    rows.append(0.0197 / 2.0 * square)
    rows.append(np.exp(-10.0 * square))
    rows += [np.zeros(LANES)] * (-len(rows) % 8)
    swap = np.zeros((LANES, LANES))
    is_real = (lane // CYCLES) % 2 == 0
    swap[lane ^ CYCLES, lane] = np.where(is_real, -1.0, 1.0)
    return np.stack(rows).astype(np.float32), swap


def spread_kernel(copies, ref_ref, out_ref, rows):
    owned = ref_ref.shape[0]
    blocks = ref_ref.shape[1] // LANES
    for o in range(owned):
        row = ref_ref[o : o + 1, :].astype(F32)
        base = o * CHUNK
        for j in range(blocks):
            rows[base + j : base + j + 1, :] = row[:, j * LANES : (j + 1) * LANES]
        rows[base + blocks : base + CHUNK, :] = jnp.zeros((CHUNK - blocks, LANES), F32)
    one = rows[...]
    out_ref[...] = jnp.concatenate([one] * copies, axis=0).astype(BF16)


def prepare_kernel(x_ref, off_ref, grp_ref, noise_ref, table_ref, swap_ref, adj_ref, turned_ref, power_ref):
    rows = x_ref.shape[0]
    noise = jnp.concatenate([noise_ref[...]] * (LANES // CYCLES), axis=1)
    defocus = 10000.0 + 1500.0 * grp_ref[...].astype(F32)
    chi_cos, chi_sin = turn_trig(defocus * table_ref[2 * HALF : 2 * HALF + 1, :])
    ctf = -(0.995 * chi_sin + 0.1 * chi_cos) * table_ref[2 * HALF + 1 : 2 * HALF + 2, :]
    scale = ctf / noise
    power_ref[...] = ctf * scale
    shift = off_ref[...].astype(F32)
    shift_x = jnp.broadcast_to(shift[:, 0:1], (rows, LANES))
    shift_y = jnp.broadcast_to(shift[:, 1:2], (rows, LANES))
    swap = swap_ref[...]
    for t in range(HALF):
        turns = shift_x * table_ref[t : t + 1, :] + shift_y * table_ref[HALF + t : HALF + t + 1, :]
        cosine, sine = turn_trig(turns)
        cosine = cosine * scale
        sine = sine * scale
        for tile, sign in ((t, 1), (t + HALF, -1)):
            x = x_ref[:, tile * LANES : (tile + 1) * LANES]
            other = jnp.dot(x, swap, preferred_element_type=F32)
            first = x.astype(F32) * cosine
            second = other * sine
            out = first + second if sign > 0 else first - second
            adj_ref[:, tile * LANES : (tile + 1) * LANES] = out.astype(BF16)
            turned_ref[tile * LANES : (tile + 1) * LANES, :] = out.T.astype(BF16)


def score_kernel(got_ref, turned_ref, power_ref, prior_ref, e_ref, best_ref, lse_ref, wide):
    classes = prior_ref.shape[0]
    particles = turned_ref.shape[1]
    wide[...] = got_ref[...].astype(F32)
    blocks = []
    ref_power = jnp.zeros((classes, LANES), F32)
    for j in range(ROT):
        block = wide[pl.ds(j, classes, stride=CHUNK), :]
        ref_power = ref_power + block * block
        blocks.append(block.astype(BF16))
    energy = 0.5 * lax.dot_general(
        ref_power, power_ref[...], (((1,), (1,)), ((), ())), precision=HIGHEST, preferred_element_type=F32
    )
    bias = prior_ref[...] - energy
    bias = jnp.concatenate([bias, bias], axis=1)
    lhs = jnp.concatenate(
        [jnp.concatenate([blocks[(i + 2 * r) % ROT] for i in range(ROT)], axis=1) for r in range(HALF)], axis=0
    )
    tiles = [turned_ref[i * LANES : (i + 1) * LANES, :] for i in range(ROT)]
    rhs = jnp.concatenate([jnp.concatenate([tiles[i], tiles[i - 1]], axis=1) for i in range(ROT)], axis=0)
    raw = jnp.dot(lhs, rhs, preferred_element_type=F32).reshape(HALF, classes, 2 * particles)
    scores = raw + bias[None]
    best = jnp.max(jnp.max(scores, axis=0), axis=0, keepdims=True)
    best = jnp.maximum(best[:, :particles], best[:, particles:])
    both = jnp.concatenate([best, best], axis=1)
    e = jnp.exp(scores - both[None])
    total = jnp.sum(jnp.sum(e, axis=0), axis=0, keepdims=True)
    total = total[:, :particles] + total[:, particles:]
    e_ref[...] = e.reshape(HALF * classes, 2 * particles)
    best_ref[...] = best
    lse_ref[...] = best + jnp.log(total)


def sum_kernel(e_ref, best_ref, lse_ref, adj_ref, power_ref, out_ref, evidence_ref, wide):
    particles = adj_ref.shape[0]
    classes = e_ref.shape[0] // HALF
    lse = lse_ref[...]
    top = jnp.max(lse, axis=0, keepdims=True)
    evidence = top + jnp.log(jnp.sum(jnp.exp(lse - top), axis=0, keepdims=True))
    evidence_ref[...] = evidence
    factor = jnp.exp(best_ref[...] - evidence)
    post = e_ref[...] * jnp.concatenate([factor, factor], axis=1)
    mass = jnp.sum(post.reshape(HALF, classes, 2 * particles), axis=0)
    mass = mass[:, :particles] + mass[:, particles:]
    weight = jnp.dot(mass, power_ref[...], precision=HIGHEST, preferred_element_type=F32)
    post = post.astype(BF16)
    blocks = [
        post[(q // 2) * classes : (q // 2 + 1) * classes, (q % 2) * particles : (q % 2 + 1) * particles]
        for q in range(ROT)
    ]
    lhs = jnp.concatenate(
        [jnp.concatenate([blocks[(2 * r - i) % ROT] for i in range(ROT)], axis=1) for r in range(HALF)], axis=0
    )
    tiles = [adj_ref[:, i * LANES : (i + 1) * LANES] for i in range(ROT)]
    rhs = jnp.concatenate(
        [jnp.concatenate([tiles[i], tiles[(i + 1) % ROT]], axis=1) for i in range(ROT)], axis=0
    )
    data = jnp.dot(lhs, rhs, preferred_element_type=F32)
    for n in range(ROT):
        r, d = n // 2, n % 2
        wide[pl.ds(n, classes, stride=CHUNK), :] = data[r * classes : (r + 1) * classes, d * LANES : (d + 1) * LANES]
    group = lax.broadcasted_iota(jnp.int32, weight.shape, 1) // CYCLES
    high = weight.astype(BF16).astype(F32)
    rest = weight - high
    middle = rest.astype(BF16).astype(F32)
    terms = jnp.where(group == 0, high, jnp.where(group == 1, middle, jnp.where(group == 2, rest - middle, 0.0)))
    wide[pl.ds(ROT, classes, stride=CHUNK), :] = terms
    for n in range(ROT + 1, CHUNK):
        wide[pl.ds(n, classes, stride=CHUNK), :] = jnp.zeros((classes, LANES), F32)
    out_ref[...] = wide[...].astype(BF16)


def final_kernel(senders, got_ref, data_ref, weight_ref):
    owned = data_ref.shape[0]
    got = got_ref[...].astype(F32).reshape(senders, owned * CHUNK, LANES)
    total = jnp.sum(got, axis=0)
    for o in range(owned):
        base = o * CHUNK
        for n in range(ROT):
            data_ref[o : o + 1, n * LANES : (n + 1) * LANES] = total[base + n : base + n + 1, :]
        terms = total[base + ROT : base + ROT + 1, :]
        weight_ref[o : o + 1, :] = (
            terms[:, :CYCLES] + terms[:, CYCLES : 2 * CYCLES] + terms[:, 2 * CYCLES : 3 * CYCLES]
        )


def call(kernel, outs, scratch=(), flops=0, bytes_accessed=0):
    return pl.pallas_call(
        kernel,
        out_shape=tuple(jax.ShapeDtypeStruct(shape, dtype) for shape, dtype in outs),
        out_specs=tuple(pl.BlockSpec(memory_space=pltpu.VMEM) for _ in outs),
        scratch_shapes=list(scratch),
        compiler_params=pltpu.CompilerParams(vmem_limit_bytes=VMEM_LIMIT),
        cost_estimate=pl.CostEstimate(flops=flops, bytes_accessed=bytes_accessed, transcendentals=0),
    )


def per_device(particles, references, log_prior, noise_var, offsets, groups):
    dom_size = lax.axis_size("dom")
    cls_size = lax.axis_size("cls")
    rows, samples = particles.shape
    owned = references.shape[0]
    classes = log_prior.shape[0]
    message = classes * CHUNK
    table, swap = lane_tables()

    (spread,) = call(
        functools.partial(spread_kernel, dom_size),
        [((message, LANES), BF16)],
        [pltpu.VMEM((owned * CHUNK, LANES), F32)],
        bytes_accessed=message * LANES * 2,
    )(references)
    got = lax.all_to_all(spread, "dom", 0, 0, tiled=True)
    adjusted, turned, power = call(
        prepare_kernel,
        [((rows, samples), BF16), ((samples, rows), BF16), ((rows, LANES), F32)],
        flops=rows * samples * 300,
        bytes_accessed=rows * samples * 6,
    )(
        particles,
        offsets,
        groups.reshape(rows, 1),
        noise_var.reshape(1, CYCLES),
        jnp.asarray(table),
        jnp.asarray(swap, BF16),
    )
    dot_flops = 2 * ROT * classes * rows * samples
    e, best, lse = call(
        score_kernel,
        [((HALF * classes, 2 * rows), F32), ((1, rows), F32), ((1, rows), F32)],
        [pltpu.VMEM((message, LANES), F32)],
        flops=dot_flops,
        bytes_accessed=rows * samples * 4,
    )(got, turned, power, log_prior.reshape(classes, 1))
    lse_all = lax.all_gather(lse, "cls", axis=0, tiled=True)
    sums, evidence = call(
        sum_kernel,
        [((message, LANES), BF16), ((1, rows), F32)],
        [pltpu.VMEM((message, LANES), F32)],
        flops=dot_flops,
        bytes_accessed=rows * samples * 4,
    )(e, best, lse_all, adjusted, power)
    mine = lax.all_to_all(sums, "dom", 0, 0, tiled=True)
    data, weight = call(
        functools.partial(final_kernel, dom_size),
        [((owned, samples), F32), ((owned, CYCLES), F32)],
        bytes_accessed=message * LANES * 2,
    )(mine)
    return data, weight, evidence.reshape(rows)


def solution(mesh):
    return jax.shard_map(
        per_device,
        mesh=mesh,
        in_specs=(P("dom", None), P(("cls", "dom"), None), P("cls"), P(), P("dom", None), P("dom")),
        out_specs=(P(("cls", "dom"), None), P(("cls", "dom"), None), P("dom")),
        check_vma=False,
    )
```

time: 314 us -> 38.6 us (0.12)
  matrix products: 77.4 us -> 0 us
  blocking collectives: 86 us -> 16.7 us
  waiting for transfers between devices: 64.8 us -> 0.01 us
  local copies, waits for them, and re-layouts: 48.3 us -> 6.4 us
  other arithmetic: 21.4 us -> 0 us
  between operations: 14.2 us -> 0.67 us
  starting transfers between devices: 0.04 us -> 8.31 us
  Pallas kernels: 0 us -> 6 us
    dot_general x26 -> x0, matrix products: 77.4 us -> none  [the longest x12 39.5 us: score_group(): jnp.einsum('cn,rpn->rcp', ref_block, rotated, preferred_element_type=jnp....]
    psum x1 -> x0, waiting for transfers between devices: 64.8 us -> none  [per_device(): data_total, weight_total = lax.psum((class_data, class_weight), 'dom')]
    all_gather x1, blocking collectives: 43.9 us -> 1.77 us  [per_device(): lse_all = lax.all_gather(lse, 'cls', axis=0, tiled=True)]
    psum x2 -> x0, blocking collectives: 39.6 us -> none  [the longest x1 37.1 us: per_device(): data_total, weight_total = lax.psum((class_data, class_weight), 'dom')]
    another operation x24 -> x0, local copies, waits for them, and re-layouts: 39.4 us -> none  [rotate_group(): return jnp.stack(pieces, axis=0)]
    all_to_all x0 -> x1, blocking collectives: none -> 14.9 us  [per_device(): mine = lax.all_to_all(sums, 'dom', 0, 0, tiled=True)]
    concatenate x1 -> x0, other arithmetic: 9.29 us -> none  [per_device(): doubled = jnp.concatenate([adjusted, adjusted], axis=1)]
    all_to_all x0 -> x1, starting transfers between devices: none -> 8.31 us  [per_device(): got = lax.all_to_all(spread, 'dom', 0, 0, tiled=True)]
  transfers between devices with their start and end apart: 1 -> 1, of which waited for: 1 -> 0; matrix products, arithmetic and copies ran while one was open for 0% -> 6% of each run, Pallas kernels for 0% -> 6%
where the time goes in v1:
time: 38.6 us; the launch traced here: 38.1 us
  blocking collectives  16.7 us (43%)
  starting transfers between devices  8.31 us (22%)
  local copies, waits for them, and re-layouts  6.4 us (17%)
  Pallas kernels  6 us (16%)
  between operations  0.67 us (2%)
    all_to_all x1, blocking collectives, per_device(): mine = lax.all_to_all(sums, 'dom', 0, 0, tiled=True)  14.9 us
    all_to_all x1, starting transfers between devices, per_device(): got = lax.all_to_all(spread, 'dom', 0, 0, tiled=True)  8.31 us
    unnamed x11, local copies, waits for them, and re-layouts  4.9 us
    pallas_call x1, Pallas kernels, per_device(): call(prepare_kernel, [((rows, samples), BF16), ((samples, rows), BF16), (...  2.4 us
    all_gather x1, blocking collectives, per_device(): lse_all = lax.all_gather(lse, 'cls', axis=0, tiled=True)  1.77 us
    pallas_call x1, Pallas kernels, per_device(): call(sum_kernel, [((message, LANES), BF16), ((1, rows), F32)], [pltpu.VME...  1.21 us
    pallas_call x1, Pallas kernels, per_device(): call(score_kernel, [((HALF * classes, 2 * rows), F32), ((1, rows), F32),...  1.07 us
  transfers between devices with their start and end apart: 1, of which 0 were waited for; matrix products, arithmetic and copies ran while one was open for 6% of the time, Pallas kernels for 6%

profile of v1, /device:TPU:0, one launch (start us, length us, event | category | flops | bytes accessed | tf_op | source)
XLA Modules:
  0.0 38.1 jit_solution(11600137368898239782)
XLA Ops:
  0.6 0.0 copy-start.3
  0.6 0.7 %copy-done.3 = bf16[1,4608]{1,0:T(2,128)(2,1)S(1)} copy-done((bf16[1,4608]{1,0:T(2,128)(2,1)S(1)}, bf16[1,4608]{1,0:T(2,128)(2,1)}, u32[]{:S(2)}) %copy-start.3) | copy-done | bytes 9240
  1.4 0.7 %shard_map.103 = bf16[640,128]{1,0:T(8,128)(2,1)} custom-call(bf16[1,4608]{1,0:T(2,128)(2,1)S(1)} %copy-done.3), custom_call_target="tpu_custom_call" | custom-call | bytes 163840 | tf_op jit(solution)/shard_map/pallas_call | solution.py:215
  2.0 8.3 %all-to-all-start = ((bf16[16,40,128]{2,1,0:T(8,128)(2,1)}), bf16[16,40,128]{2,1,0:T(8,128)(2,1)S(1)}, u32[]{:S(2)}, u32[]{:S(2)}) async-start(bf16[16,40,128]{2,1,0:T(8,128)(2,1)} %bitcast), calls=%async_computation | async-start | bytes 327680 | tf_op jit(solution)/shard_map/all_to_all | solution.py:221
  10.4 0.7 %copy.17.prior_ref = f32[16,1]{1,0:T(8,128)S(1)} copy(f32[16,1]{0,1:T(1,128)} %bitcast.17) | data formatting | bytes 128 | tf_op jit(solution)/shard_map/reshape | solution.py:242
  11.1 0.8 %copy.15.off_ref = s32[128,2]{1,0:T(8,128)S(1)} copy(s32[128,2]{0,1:T(2,128)} %param.12) | data formatting | bytes 2048 | tf_op args[4]
  11.9 0.8 %copy.16.grp_ref = s32[128,1]{1,0:T(8,128)S(1)} copy(s32[128,1]{0,1:T(1,128)} %bitcast.16) | data formatting | bytes 1024 | tf_op jit(solution)/shard_map/reshape | solution.py:230
  12.6 0.0 copy-start
  12.6 1.3 %copy-done = bf16[128,4608]{1,0:T(8,128)(2,1)S(1)} copy-done((bf16[128,4608]{1,0:T(8,128)(2,1)S(1)}, bf16[128,4608]{1,0:T(8,128)(2,1)}, u32[]{:S(2)}) %copy-start) | copy-done | bytes 1179672
  13.9 0.0 copy-start.1
  13.9 0.8 %copy-done.1 = bf16[128,128]{1,0:T(8,128)(2,1)S(1)} copy-done((bf16[128,128]{1,0:T(8,128)(2,1)S(1)}, bf16[128,128]{1,0:T(8,128)(2,1)}, u32[]{:S(2)}) %copy-start.1) | copy-done | bytes 32792
  14.7 0.0 copy-start.2
  14.7 0.7 %copy-done.2 = f32[40,128]{1,0:T(8,128)S(1)} copy-done((f32[40,128]{1,0:T(8,128)S(1)}, f32[40,128]{1,0:T(8,128)}, u32[]{:S(2)}) %copy-start.2) | copy-done | bytes 20504
  15.4 0.0 copy-start.4
  15.4 0.7 %copy-done.4 = f32[32]{0:T(128)S(1)} copy-done((f32[32]{0:T(128)S(1)}, f32[32]{0:T(128)}, u32[]{:S(2)}) %copy-start.4) | copy-done | bytes 152
  16.1 2.4 %shard_map.104 = (bf16[128,4608]{1,0:T(8,128)(2,1)S(1)}, bf16[4608,128]{1,0:T(8,128)(2,1)S(1)}, f32[128,128]{1,0:T(8,128)S(1)}) custom-call(bf16[128,4608]{1,0:T(8,128)(2,1)S(1)} %copy-done, s32[128,2]{1,0:T(8,128)S(1)} %copy.15.off_ref, s32[128,1]{1,0:T(8,128)S(1)} %copy.16.grp_ref, f32[1,32]{1,0:T(1,128)S(1)} %bitcast.13, f32[40,128]{1,0:T(8,128)S(1)} %copy-done.2, ...), custom_call_target="tpu_custom_call" | custom-call | flops 176947200 | bytes 3538944 | tf_op jit(solution)/shard_map/pallas_call | solution.py:222
  18.4 0.0 all-to-all-done
  18.5 1.1 %shard_map.105 = (f32[288,256]{1,0:T(8,128)S(1)}, f32[1,128]{1,0:T(1,128)S(1)}, f32[1,128]{1,0:T(1,128)S(1)}) custom-call(bf16[640,128]{1,0:T(8,128)(2,1)S(1)} %bitcast.11, bf16[4608,128]{1,0:T(8,128)(2,1)S(1)} %get-tuple-element.13.turned_ref, f32[128,128]{1,0:T(8,128)S(1)} %get-tuple-element.14.power_ref, f32[16,1]{1,0:T(8,128)S(1)} %copy.17.prior_ref), custom_call_target="tpu_custom_call" | custom-call | flops 679477248 | bytes 2359296 | tf_op jit(solution)/shard_map/pallas_call | solution.py:236
  19.5 1.8 %all-gather = f32[2,1,128]{2,1,0:T(1,128)S(1)} all-gather(f32[1,1,128]{2,1,0:T(1,128)S(1)} %bitcast.15), channel_id=1, replica_groups=mesh['dom'=16,'cls'=2] {'cls'}, dimensions={0}, use_global_device_ids=true | all-gather | bytes 1536 | tf_op jit(solution)/shard_map/all_gather | solution.py:243
  21.3 1.2 %shard_map.106 = (bf16[640,128]{1,0:T(8,128)(2,1)S(1)}, f32[1,128]{1,0:T(1,128)}) custom-call(f32[288,256]{1,0:T(8,128)S(1)} %get-tuple-element.15.e_ref, f32[1,128]{1,0:T(1,128)S(1)} %get-tuple-element.16.best_ref, f32[2,128]{1,0:T(2,128)S(1)} %bitcast.14, bf16[128,4608]{1,0:T(8,128)(2,1)S(1)} %get-tuple-element.18.adj_ref, ...), custom_call_target="tpu_custom_call" | custom-call | flops 679477248 | bytes 2359296 | tf_op jit(solution)/shard_map/pallas_call | solution.py:244
  22.5 14.9 %all_to_all.22 = bf16[16,40,128]{2,1,0:T(8,128)(2,1)S(1)} all-to-all(bf16[16,40,128]{2,1,0:T(8,128)(2,1)S(1)} %bitcast.12), channel_id=1, replica_groups=mesh['dom'=16,'cls'=2] {'dom'}, dimensions={0} | all-to-all | bytes 327680 | tf_op jit(solution)/shard_map/all_to_all | solution.py:251
  37.4 0.6 %shard_map.107 = (f32[1,4608]{1,0:T(1,128)}, f32[1,32]{1,0:T(1,128)}) custom-call(bf16[640,128]{1,0:T(8,128)(2,1)S(1)} %bitcast.10), custom_call_target="tpu_custom_call" | custom-call | bytes 163840 | tf_op jit(solution)/shard_map/pallas_call | solution.py:252
Async XLA Ops:
  0.6 0.7 %copy-start.3 = (bf16[1,4608]{1,0:T(2,128)(2,1)S(1)}, bf16[1,4608]{1,0:T(2,128)(2,1)}, u32[]{:S(2)}) copy-start(bf16[1,4608]{1,0:T(2,128)(2,1)} %ref_ref.1) | copy-start | bytes 27652
  2.0 16.4 %all-to-all-start = ((bf16[16,40,128]{2,1,0:T(8,128)(2,1)}), bf16[16,40,128]{2,1,0:T(8,128)(2,1)S(1)}, u32[]{:S(2)}, u32[]{:S(2)}) async-start(bf16[16,40,128]{2,1,0:T(8,128)(2,1)} %bitcast), calls=%async_computation | async-start | bytes 327680 | tf_op jit(solution)/shard_map/all_to_all | solution.py:221
  12.6 1.3 %copy-start = (bf16[128,4608]{1,0:T(8,128)(2,1)S(1)}, bf16[128,4608]{1,0:T(8,128)(2,1)}, u32[]{:S(2)}) copy-start(bf16[128,4608]{1,0:T(8,128)(2,1)} %x_ref.1) | copy-start | bytes 3538948
  13.9 0.8 %copy-start.1 = (bf16[128,128]{1,0:T(8,128)(2,1)S(1)}, bf16[128,128]{1,0:T(8,128)(2,1)}, u32[]{:S(2)}) copy-start(bf16[128,128]{1,0:T(8,128)(2,1)} %constant.5.clone.swap_ref) | copy-start | bytes 98308
  14.7 0.7 %copy-start.2 = (f32[40,128]{1,0:T(8,128)S(1)}, f32[40,128]{1,0:T(8,128)}, u32[]{:S(2)}) copy-start(f32[40,128]{1,0:T(8,128)} %constant.4.clone.table_ref) | copy-start | bytes 61444
  15.4 0.7 %copy-start.4 = (f32[32]{0:T(128)S(1)}, f32[32]{0:T(128)}, u32[]{:S(2)}) copy-start(f32[32]{0:T(128)} %param.11) | copy-start | bytes 388

commit v2 on v1

--- a/solution.py
+++ b/solution.py
@@ -15,6 +15,7 @@
 ANGLES = 72
 LANES = 128
 HALF = ROT // 2
+GROUP = 3
 CHUNK = 40
 F32 = jnp.float32
 BF16 = jnp.bfloat16
@@ -60,10 +61,7 @@
     rows.append(0.0197 / 2.0 * square)
     rows.append(np.exp(-10.0 * square))
     rows += [np.zeros(LANES)] * (-len(rows) % 8)
-    swap = np.zeros((LANES, LANES))
-    is_real = (lane // CYCLES) % 2 == 0
-    swap[lane ^ CYCLES, lane] = np.where(is_real, -1.0, 1.0)
-    return np.stack(rows).astype(np.float32), swap
+    return np.stack(rows).astype(np.float32)
 
 
 def spread_kernel(copies, ref_ref, out_ref, rows):
@@ -79,19 +77,52 @@
     out_ref[...] = jnp.concatenate([one] * copies, axis=0).astype(BF16)
 
 
-def prepare_kernel(x_ref, off_ref, grp_ref, noise_ref, table_ref, swap_ref, adj_ref, turned_ref, power_ref):
+def prepare_kernel(
+    x_hbm, off_hbm, grp_hbm, noise_hbm, table_hbm, adj_ref, turned_ref, power_ref, x_ref, off_ref, grp_ref, noise_ref,
+    table_ref, small_sems, x_sems
+):
     rows = x_ref.shape[0]
+    width = GROUP * LANES
+    small = [
+        pltpu.make_async_copy(source, target, small_sems.at[i])
+        for i, (source, target) in enumerate(
+            ((off_hbm, off_ref), (grp_hbm, grp_ref), (noise_hbm, noise_ref), (table_hbm, table_ref))
+        )
+    ]
+    for copy in small:
+        copy.start()
+    parts = []
+    for g in range(2 * HALF // GROUP):
+        part = slice((g // 2 + g % 2 * (HALF // GROUP)) * width, (g // 2 + g % 2 * (HALF // GROUP) + 1) * width)
+        copy = pltpu.make_async_copy(x_hbm.at[:, part], x_ref.at[:, part], x_sems.at[g])
+        copy.start()
+        parts.append(copy)
+    out_lane = lax.broadcasted_iota(jnp.int32, (LANES, LANES), 1)
+    in_lane = lax.broadcasted_iota(jnp.int32, (LANES, LANES), 0)
+    is_real = (out_lane // CYCLES) % 2 == 0
+    swap = jnp.where(
+        is_real,
+        jnp.where(in_lane == out_lane + CYCLES, -1.0, 0.0),
+        jnp.where(in_lane == out_lane - CYCLES, 1.0, 0.0),
+    ).astype(BF16)
+    for copy in small:
+        copy.wait()
     noise = jnp.concatenate([noise_ref[...]] * (LANES // CYCLES), axis=1)
-    defocus = 10000.0 + 1500.0 * grp_ref[...].astype(F32)
+
+    def down(row):
+        return jnp.broadcast_to(row.astype(F32), (LANES, rows)).T
+
+    defocus = 10000.0 + 1500.0 * down(grp_ref[...])
     chi_cos, chi_sin = turn_trig(defocus * table_ref[2 * HALF : 2 * HALF + 1, :])
     ctf = -(0.995 * chi_sin + 0.1 * chi_cos) * table_ref[2 * HALF + 1 : 2 * HALF + 2, :]
     scale = ctf / noise
     power_ref[...] = ctf * scale
-    shift = off_ref[...].astype(F32)
-    shift_x = jnp.broadcast_to(shift[:, 0:1], (rows, LANES))
-    shift_y = jnp.broadcast_to(shift[:, 1:2], (rows, LANES))
-    swap = swap_ref[...]
+    shift_x = down(off_ref[0:1, :])
+    shift_y = down(off_ref[1:2, :])
     for t in range(HALF):
+        if t % GROUP == 0:
+            for copy in parts[2 * (t // GROUP) : 2 * (t // GROUP) + 2]:
+                copy.wait()
         turns = shift_x * table_ref[t : t + 1, :] + shift_y * table_ref[HALF + t : HALF + t + 1, :]
         cosine, sine = turn_trig(turns)
         cosine = cosine * scale
@@ -107,8 +138,12 @@
 
 
 def score_kernel(got_ref, turned_ref, power_ref, prior_ref, e_ref, best_ref, lse_ref, wide):
-    classes = prior_ref.shape[0]
+    classes = prior_ref.shape[1]
     particles = turned_ref.shape[1]
+    diagonal = lax.broadcasted_iota(jnp.int32, (classes, classes), 0) == lax.broadcasted_iota(
+        jnp.int32, (classes, classes), 1
+    )
+    prior = jnp.sum(jnp.where(diagonal, jnp.broadcast_to(prior_ref[...], (classes, classes)), 0.0), axis=1, keepdims=True)
     wide[...] = got_ref[...].astype(F32)
     blocks = []
     ref_power = jnp.zeros((classes, LANES), F32)
@@ -119,7 +154,7 @@
     energy = 0.5 * lax.dot_general(
         ref_power, power_ref[...], (((1,), (1,)), ((), ())), precision=HIGHEST, preferred_element_type=F32
     )
-    bias = prior_ref[...] - energy
+    bias = prior - energy
     bias = jnp.concatenate([bias, bias], axis=1)
     lhs = jnp.concatenate(
         [jnp.concatenate([blocks[(i + 2 * r) % ROT] for i in range(ROT)], axis=1) for r in range(HALF)], axis=0
@@ -139,10 +174,11 @@
     lse_ref[...] = best + jnp.log(total)
 
 
-def sum_kernel(e_ref, best_ref, lse_ref, adj_ref, power_ref, out_ref, evidence_ref, wide):
+def sum_kernel(e_ref, best_ref, adj_ref, power_ref, *rest):
+    *lse_refs, out_ref, evidence_ref, wide = rest
     particles = adj_ref.shape[0]
     classes = e_ref.shape[0] // HALF
-    lse = lse_ref[...]
+    lse = jnp.concatenate([ref[...] for ref in lse_refs], axis=0)
     top = jnp.max(lse, axis=0, keepdims=True)
     evidence = top + jnp.log(jnp.sum(jnp.exp(lse - top), axis=0, keepdims=True))
     evidence_ref[...] = evidence
@@ -192,15 +228,20 @@
         )
 
 
-def call(kernel, outs, scratch=(), flops=0, bytes_accessed=0):
-    return pl.pallas_call(
-        kernel,
-        out_shape=tuple(jax.ShapeDtypeStruct(shape, dtype) for shape, dtype in outs),
-        out_specs=tuple(pl.BlockSpec(memory_space=pltpu.VMEM) for _ in outs),
-        scratch_shapes=list(scratch),
-        compiler_params=pltpu.CompilerParams(vmem_limit_bytes=VMEM_LIMIT),
-        cost_estimate=pl.CostEstimate(flops=flops, bytes_accessed=bytes_accessed, transcendentals=0),
-    )
+def call(kernel, outs, scratch=(), in_hbm=(), flops=0, bytes_accessed=0):
+    def run(*args):
+        args = [pltpu.with_memory_space_constraint(x, pltpu.HBM) if i in in_hbm else x for i, x in enumerate(args)]
+        return pl.pallas_call(
+            kernel,
+            out_shape=tuple(jax.ShapeDtypeStruct(shape, dtype) for shape, dtype in outs),
+            in_specs=[pl.BlockSpec(memory_space=pltpu.HBM if i in in_hbm else pltpu.VMEM) for i in range(len(args))],
+            out_specs=tuple(pl.BlockSpec(memory_space=pltpu.VMEM) for _ in outs),
+            scratch_shapes=list(scratch),
+            compiler_params=pltpu.CompilerParams(vmem_limit_bytes=VMEM_LIMIT),
+            cost_estimate=pl.CostEstimate(flops=flops, bytes_accessed=bytes_accessed, transcendentals=0),
+        )(*args)
+
+    return run
 
 
 def per_device(particles, references, log_prior, noise_var, offsets, groups):
@@ -210,7 +251,7 @@
     owned = references.shape[0]
     classes = log_prior.shape[0]
     message = classes * CHUNK
-    table, swap = lane_tables()
+    table = lane_tables()
 
     (spread,) = call(
         functools.partial(spread_kernel, dom_size),
@@ -222,16 +263,19 @@
     adjusted, turned, power = call(
         prepare_kernel,
         [((rows, samples), BF16), ((samples, rows), BF16), ((rows, LANES), F32)],
+        [
+            pltpu.VMEM((rows, samples), BF16),
+            pltpu.VMEM((2, rows), jnp.int32),
+            pltpu.VMEM((1, rows), jnp.int32),
+            pltpu.VMEM((1, CYCLES), F32),
+            pltpu.VMEM(table.shape, F32),
+            pltpu.SemaphoreType.DMA((4,)),
+            pltpu.SemaphoreType.DMA((2 * HALF // GROUP,)),
+        ],
+        in_hbm=range(5),
         flops=rows * samples * 300,
         bytes_accessed=rows * samples * 6,
-    )(
-        particles,
-        offsets,
-        groups.reshape(rows, 1),
-        noise_var.reshape(1, CYCLES),
-        jnp.asarray(table),
-        jnp.asarray(swap, BF16),
-    )
+    )(particles, offsets.T, groups.reshape(1, rows), noise_var.reshape(1, CYCLES), jnp.asarray(table))
     dot_flops = 2 * ROT * classes * rows * samples
     e, best, lse = call(
         score_kernel,
@@ -239,15 +283,18 @@
         [pltpu.VMEM((message, LANES), F32)],
         flops=dot_flops,
         bytes_accessed=rows * samples * 4,
-    )(got, turned, power, log_prior.reshape(classes, 1))
-    lse_all = lax.all_gather(lse, "cls", axis=0, tiled=True)
+    )(got, turned, power, log_prior.reshape(1, classes))
+    if cls_size == 2:
+        all_lse = (lse, lax.ppermute(lse, "cls", [(0, 1), (1, 0)]))
+    else:
+        all_lse = (lax.all_gather(lse, "cls", axis=0, tiled=True),)
     sums, evidence = call(
         sum_kernel,
         [((message, LANES), BF16), ((1, rows), F32)],
         [pltpu.VMEM((message, LANES), F32)],
         flops=dot_flops,
         bytes_accessed=rows * samples * 4,
-    )(e, best, lse_all, adjusted, power)
+    )(e, best, adjusted, power, *all_lse)
     mine = lax.all_to_all(sums, "dom", 0, 0, tiled=True)
     data, weight = call(
         functools.partial(final_kernel, dom_size),

time: 38.6 us -> 34.1 us (0.88)
  local copies, waits for them, and re-layouts: 6.4 us -> 0.72 us
  blocking collectives: 16.7 us -> 11.4 us
  waiting for transfers between devices: 0.01 us -> 4.83 us
  Pallas kernels: 6 us -> 7.8 us
    unnamed x11 -> x4, local copies, waits for them, and re-layouts: 4.9 us -> 0.72 us
    all_to_all x1, waiting for transfers between devices: 0.01 us -> 3.72 us  [per_device(): got = lax.all_to_all(spread, 'dom', 0, 0, tiled=True)]
    all_to_all x1, blocking collectives: 14.9 us -> 11.4 us  [per_device(): mine = lax.all_to_all(sums, 'dom', 0, 0, tiled=True)]
    pallas_call x5, Pallas kernels: 6 us -> 7.8 us  [run(): pl.pallas_call(kernel, out_shape=tuple((jax.ShapeDtypeStruct(shape, dtype...]
    all_gather x1 -> x0, blocking collectives: 1.77 us -> none  [per_device(): lse_all = lax.all_gather(lse, 'cls', axis=0, tiled=True)]
    reshape x2 -> x0, local copies, waits for them, and re-layouts: 1.49 us -> none  [the longest x1 0.76 us: per_device(): groups.reshape(rows, 1)]
    ppermute x0 -> x1, waiting for transfers between devices: none -> 1.11 us  [per_device(): all_lse = (lse, lax.ppermute(lse, 'cls', [(0, 1), (1, 0)]))]
  transfers between devices with their start and end apart: 1 -> 2, of which waited for: 0 -> 2; matrix products, arithmetic and copies ran while one was open for 6% -> 0% of each run, Pallas kernels for 6% -> 12%
where the time goes in v2:
time: 34.1 us; the launch traced here: 33.8 us
  blocking collectives  11.4 us (33%)
  starting transfers between devices  8.38 us (25%)
  Pallas kernels  7.8 us (23%)
  waiting for transfers between devices  4.83 us (14%)
  local copies, waits for them, and re-layouts  0.72 us (2%)
  between operations  0.67 us (2%)
    all_to_all x1, blocking collectives, per_device(): mine = lax.all_to_all(sums, 'dom', 0, 0, tiled=True)  11.4 us
    all_to_all x1, starting transfers between devices, per_device(): got = lax.all_to_all(spread, 'dom', 0, 0, tiled=True)  8.31 us
    pallas_call x5, Pallas kernels, run(): pl.pallas_call(kernel, out_shape=tuple((jax.ShapeDtypeStruct(shape, dtype...  7.8 us
    all_to_all x1, waiting for transfers between devices, per_device(): got = lax.all_to_all(spread, 'dom', 0, 0, tiled=True)  3.72 us
    ppermute x1, waiting for transfers between devices, per_device(): all_lse = (lse, lax.ppermute(lse, 'cls', [(0, 1), (1, 0)]))  1.11 us
    unnamed x4, local copies, waits for them, and re-layouts  0.72 us
  transfers between devices with their start and end apart: 2, of which 2 were waited for; matrix products, arithmetic and copies ran while one was open for 0% of the time, Pallas kernels for 12%

profile of v2, /device:TPU:0, one launch (start us, length us, event | category | flops | bytes accessed | tf_op | source)
XLA Modules:
  0.0 33.8 jit_solution(6343788654856257586)
XLA Ops:
  0.6 0.0 copy-start
  0.6 0.7 %copy-done = bf16[1,4608]{1,0:T(2,128)(2,1)S(1)} copy-done((bf16[1,4608]{1,0:T(2,128)(2,1)S(1)}, bf16[1,4608]{1,0:T(2,128)(2,1)}, u32[]{:S(2)}) %copy-start) | copy-done | bytes 9240
  1.4 0.0 copy-start.1
  1.4 0.7 %shard_map.94 = bf16[640,128]{1,0:T(8,128)(2,1)} custom-call(bf16[1,4608]{1,0:T(2,128)(2,1)S(1)} %copy-done), custom_call_target="tpu_custom_call" | custom-call | bytes 163840 | tf_op jit(solution)/shard_map/pallas_call | solution.py:234
  2.0 8.3 %all-to-all-start = ((bf16[16,40,128]{2,1,0:T(8,128)(2,1)}), bf16[16,40,128]{2,1,0:T(8,128)(2,1)S(1)}, u32[]{:S(2)}, u32[]{:S(2)}) async-start(bf16[16,40,128]{2,1,0:T(8,128)(2,1)} %bitcast), calls=%async_computation | async-start | bytes 327680 | tf_op jit(solution)/shard_map/all_to_all | solution.py:262
  10.4 4.2 %shard_map.95 = (bf16[128,4608]{1,0:T(8,128)(2,1)S(1)}, bf16[4608,128]{1,0:T(8,128)(2,1)S(1)}, f32[128,128]{1,0:T(8,128)S(1)}) custom-call(bf16[128,4608]{1,0:T(8,128)(2,1)} %x_hbm.1, s32[2,128]{1,0:T(2,128)} %bitcast.13, s32[1,128]{1,0:T(1,128)} %bitcast.14, f32[1,32]{1,0:T(1,128)} %bitcast.15, f32[40,128]{1,0:T(8,128)} %constant.2.clone.table_hbm), custom_call_target="tpu_custom_call" | custom-call | flops 176947200 | bytes 3538944 | tf_op jit(solution)/shard_map/pallas_call | solution.py:234
  14.6 3.7 %all-to-all-done = bf16[16,40,128]{2,1,0:T(8,128)(2,1)S(1)} async-done(((bf16[16,40,128]{2,1,0:T(8,128)(2,1)}), bf16[16,40,128]{2,1,0:T(8,128)(2,1)S(1)}, u32[]{:S(2)}, u32[]{:S(2)}) %all-to-all-start) | async-done | bytes 163872 | tf_op jit(solution)/shard_map/all_to_all | solution.py:262
  18.3 0.0 copy-done.1
  18.3 1.1 %shard_map.96 = (f32[288,256]{1,0:T(8,128)S(1)}, f32[1,128]{1,0:T(1,128)S(1)}, f32[1,128]{1,0:T(1,128)S(1)}) custom-call(bf16[640,128]{1,0:T(8,128)(2,1)S(1)} %bitcast.10, bf16[4608,128]{1,0:T(8,128)(2,1)S(1)} %get-tuple-element.13.turned_ref, f32[128,128]{1,0:T(8,128)S(1)} %get-tuple-element.14.power_ref, f32[1,16]{1,0:T(1,128)S(1)} %bitcast.12), custom_call_target="tpu_custom_call" | custom-call | flops 679477248 | bytes 2359296 | tf_op jit(solution)/shard_map/pallas_call | solution.py:234
  19.4 0.1 collective-permute-start
  19.4 1.1 %collective-permute-done.rest_1_ = f32[1,128]{1,0:T(1,128)S(1)} collective-permute-done((f32[1,128]{1,0:T(1,128)S(1)}, f32[1,128]{1,0:T(1,128)S(1)}, u32[]{:S(2)}, u32[]{:S(2)}) %collective-permute-start) | collective-permute-done | bytes 544 | tf_op jit(solution)/shard_map/ppermute | solution.py:288
  20.5 1.2 %shard_map.97 = (bf16[640,128]{1,0:T(8,128)(2,1)S(1)}, f32[1,128]{1,0:T(1,128)}) custom-call(f32[288,256]{1,0:T(8,128)S(1)} %get-tuple-element.15.e_ref, f32[1,128]{1,0:T(1,128)S(1)} %get-tuple-element.16.best_ref, bf16[128,4608]{1,0:T(8,128)(2,1)S(1)} %get-tuple-element.17.adj_ref, f32[128,128]{1,0:T(8,128)S(1)} %get-tuple-element.14.power_ref, ...), custom_call_target="tpu_custom_call" | custom-call | flops 679477248 | bytes 2359296 | tf_op jit(solution)/shard_map/pallas_call | solution.py:234
  21.8 11.4 %all_to_all.22 = bf16[16,40,128]{2,1,0:T(8,128)(2,1)S(1)} all-to-all(bf16[16,40,128]{2,1,0:T(8,128)(2,1)S(1)} %bitcast.11), channel_id=1, replica_groups=mesh['dom'=16,'cls'=2] {'dom'}, dimensions={0} | all-to-all | bytes 327680 | tf_op jit(solution)/shard_map/all_to_all | solution.py:298
  33.1 0.6 %shard_map.98 = (f32[1,4608]{1,0:T(1,128)}, f32[1,32]{1,0:T(1,128)}) custom-call(bf16[640,128]{1,0:T(8,128)(2,1)S(1)} %bitcast.9), custom_call_target="tpu_custom_call" | custom-call | bytes 163840 | tf_op jit(solution)/shard_map/pallas_call | solution.py:234
Async XLA Ops:
  0.6 0.7 %copy-start = (bf16[1,4608]{1,0:T(2,128)(2,1)S(1)}, bf16[1,4608]{1,0:T(2,128)(2,1)}, u32[]{:S(2)}) copy-start(bf16[1,4608]{1,0:T(2,128)(2,1)} %ref_ref.1) | copy-start | bytes 27652
  1.4 16.9 %copy-start.1 = (f32[16]{0:T(128)S(1)}, f32[16]{0:T(128)}, u32[]{:S(2)}) copy-start(f32[16]{0:T(128)} %param.9) | copy-start | bytes 196
  2.0 16.3 %all-to-all-start = ((bf16[16,40,128]{2,1,0:T(8,128)(2,1)}), bf16[16,40,128]{2,1,0:T(8,128)(2,1)S(1)}, u32[]{:S(2)}, u32[]{:S(2)}) async-start(bf16[16,40,128]{2,1,0:T(8,128)(2,1)} %bitcast), calls=%async_computation | async-start | bytes 327680 | tf_op jit(solution)/shard_map/all_to_all | solution.py:262
  19.4 1.2 %collective-permute-start = (f32[1,128]{1,0:T(1,128)S(1)}, f32[1,128]{1,0:T(1,128)S(1)}, u32[]{:S(2)}, u32[]{:S(2)}) collective-permute-start(f32[1,128]{1,0:T(1,128)S(1)} %get-tuple-element.18.rest_0_), channel_id=1, source_target_pairs={{0,1},{1,0},{2,3},{3,2},{4,5},{5,4},{6,7},{7,6},{8,9},{9,8},{10,11... | collective-permute-start | bytes 1544 | tf_op jit(solution)/shard_map/ppermute | solution.py:288

commit v3 on v2

--- a/solution.py
+++ b/solution.py
@@ -64,17 +64,28 @@
     return np.stack(rows).astype(np.float32)
 
 
-def spread_kernel(copies, ref_ref, out_ref, rows):
-    owned = ref_ref.shape[0]
-    blocks = ref_ref.shape[1] // LANES
+def spread_kernel(ref_hbm, out_hbm, ref, rows, packed, in_sem, out_sems):
+    copy = pltpu.make_async_copy(ref_hbm, ref, in_sem)
+    copy.start()
+    owned = ref.shape[0]
+    blocks = ref.shape[1] // LANES
     for o in range(owned):
-        row = ref_ref[o : o + 1, :].astype(F32)
-        base = o * CHUNK
+        rows[o * CHUNK + blocks : (o + 1) * CHUNK, :] = jnp.zeros((CHUNK - blocks, LANES), F32)
+    copy.wait()
+    for o in range(owned):
+        row = ref[o : o + 1, :].astype(F32)
         for j in range(blocks):
-            rows[base + j : base + j + 1, :] = row[:, j * LANES : (j + 1) * LANES]
-        rows[base + blocks : base + CHUNK, :] = jnp.zeros((CHUNK - blocks, LANES), F32)
-    one = rows[...]
-    out_ref[...] = jnp.concatenate([one] * copies, axis=0).astype(BF16)
+            rows[o * CHUNK + j : o * CHUNK + j + 1, :] = row[:, j * LANES : (j + 1) * LANES]
+    unit = packed.shape[0]
+    packed[...] = jnp.concatenate([rows[...]] * (unit // rows.shape[0]), axis=0).astype(BF16)
+    copies = [
+        pltpu.make_async_copy(packed, out_hbm.at[i * unit : (i + 1) * unit, :], out_sems.at[i])
+        for i in range(out_hbm.shape[0] // unit)
+    ]
+    for copy in copies:
+        copy.start()
+    for copy in copies:
+        copy.wait()
 
 
 def prepare_kernel(
@@ -137,13 +148,13 @@
             turned_ref[tile * LANES : (tile + 1) * LANES, :] = out.T.astype(BF16)
 
 
-def score_kernel(got_ref, turned_ref, power_ref, prior_ref, e_ref, best_ref, lse_ref, wide):
+def score_kernel(first, got_ref, turned_ref, power_ref, prior_ref, e_ref, best_ref, lse_ref, wide):
     classes = prior_ref.shape[1]
     particles = turned_ref.shape[1]
-    diagonal = lax.broadcasted_iota(jnp.int32, (classes, classes), 0) == lax.broadcasted_iota(
-        jnp.int32, (classes, classes), 1
-    )
-    prior = jnp.sum(jnp.where(diagonal, jnp.broadcast_to(prior_ref[...], (classes, classes)), 0.0), axis=1, keepdims=True)
+    place = lax.broadcasted_iota(jnp.int32, (classes, classes), 0) + first
+    place = jnp.where(place >= classes, place - classes, place)
+    held = place == lax.broadcasted_iota(jnp.int32, (classes, classes), 1)
+    prior = jnp.sum(jnp.where(held, jnp.broadcast_to(prior_ref[...], (classes, classes)), 0.0), axis=1, keepdims=True)
     wide[...] = got_ref[...].astype(F32)
     blocks = []
     ref_power = jnp.zeros((classes, LANES), F32)
@@ -228,14 +239,14 @@
         )
 
 
-def call(kernel, outs, scratch=(), in_hbm=(), flops=0, bytes_accessed=0):
+def call(kernel, outs, scratch=(), in_hbm=(), out_space=pltpu.VMEM, flops=0, bytes_accessed=0):
     def run(*args):
         args = [pltpu.with_memory_space_constraint(x, pltpu.HBM) if i in in_hbm else x for i, x in enumerate(args)]
         return pl.pallas_call(
             kernel,
             out_shape=tuple(jax.ShapeDtypeStruct(shape, dtype) for shape, dtype in outs),
             in_specs=[pl.BlockSpec(memory_space=pltpu.HBM if i in in_hbm else pltpu.VMEM) for i in range(len(args))],
-            out_specs=tuple(pl.BlockSpec(memory_space=pltpu.VMEM) for _ in outs),
+            out_specs=tuple(pl.BlockSpec(memory_space=out_space) for _ in outs),
             scratch_shapes=list(scratch),
             compiler_params=pltpu.CompilerParams(vmem_limit_bytes=VMEM_LIMIT),
             cost_estimate=pl.CostEstimate(flops=flops, bytes_accessed=bytes_accessed, transcendentals=0),
@@ -253,13 +264,31 @@
     message = classes * CHUNK
     table = lane_tables()
 
+    root = dom_size * 3 // 4 - 1
+    exchange = functools.partial(
+        lax.all_to_all,
+        axis_name="dom",
+        split_axis=0,
+        concat_axis=0,
+        axis_index_groups=[[(i + root) % dom_size for i in range(dom_size)]],
+        tiled=True,
+    )
+    unit = math.lcm(owned * CHUNK, 16)
     (spread,) = call(
-        functools.partial(spread_kernel, dom_size),
+        spread_kernel,
         [((message, LANES), BF16)],
-        [pltpu.VMEM((owned * CHUNK, LANES), F32)],
+        [
+            pltpu.VMEM((owned, samples), BF16),
+            pltpu.VMEM((owned * CHUNK, LANES), F32),
+            pltpu.VMEM((unit, LANES), BF16),
+            pltpu.SemaphoreType.DMA,
+            pltpu.SemaphoreType.DMA((message // unit,)),
+        ],
+        in_hbm=(0,),
+        out_space=pl.ANY,
         bytes_accessed=message * LANES * 2,
     )(references)
-    got = lax.all_to_all(spread, "dom", 0, 0, tiled=True)
+    got = exchange(spread)
     adjusted, turned, power = call(
         prepare_kernel,
         [((rows, samples), BF16), ((samples, rows), BF16), ((rows, LANES), F32)],
@@ -278,7 +307,7 @@
     )(particles, offsets.T, groups.reshape(1, rows), noise_var.reshape(1, CYCLES), jnp.asarray(table))
     dot_flops = 2 * ROT * classes * rows * samples
     e, best, lse = call(
-        score_kernel,
+        functools.partial(score_kernel, root * owned),
         [((HALF * classes, 2 * rows), F32), ((1, rows), F32), ((1, rows), F32)],
         [pltpu.VMEM((message, LANES), F32)],
         flops=dot_flops,
@@ -295,7 +324,7 @@
         flops=dot_flops,
         bytes_accessed=rows * samples * 4,
     )(e, best, adjusted, power, *all_lse)
-    mine = lax.all_to_all(sums, "dom", 0, 0, tiled=True)
+    mine = exchange(sums)
     data, weight = call(
         functools.partial(final_kernel, dom_size),
         [((owned, samples), F32), ((owned, CYCLES), F32)],

time: 34.1 us -> 31.4 us (0.921)
  waiting for transfers between devices: 4.83 us -> 1.59 us
  starting transfers between devices: 8.38 us -> 9.33 us
  Pallas kernels: 7.8 us -> 8.6 us
  local copies, waits for them, and re-layouts: 0.72 us -> 0.01 us
  blocking collectives: 11.4 us -> 10.8 us
    all_to_all x1, waiting for transfers between devices: 3.72 us -> 0.48 us  [per_device(): got = exchange(spread)]
    all_to_all x1, starting transfers between devices: 8.31 us -> 9.26 us  [per_device(): got = exchange(spread)]
    pallas_call x5, Pallas kernels: 7.8 us -> 8.6 us  [run(): pl.pallas_call(kernel, out_shape=tuple((jax.ShapeDtypeStruct(shape, dtype...]
    unnamed x4 -> x2, local copies, waits for them, and re-layouts: 0.72 us -> 0.01 us
    all_to_all x1, blocking collectives: 11.4 us -> 10.8 us  [per_device(): mine = exchange(sums)]
  transfers between devices with their start and end apart: 2 -> 2, of which waited for: 2 -> 2; matrix products, arithmetic and copies ran while one was open for 0% -> 0% of each run, Pallas kernels for 12% -> 14%
where the time goes in v3:
time: 31.4 us; the launch traced here: 31 us
  blocking collectives  10.8 us (34%)
  starting transfers between devices  9.33 us (30%)
  Pallas kernels  8.6 us (27%)
  waiting for transfers between devices  1.59 us (5%)
  between operations  0.67 us (2%)
    all_to_all x1, blocking collectives, per_device(): mine = exchange(sums)  10.8 us
    all_to_all x1, starting transfers between devices, per_device(): got = exchange(spread)  9.26 us
    pallas_call x5, Pallas kernels, run(): pl.pallas_call(kernel, out_shape=tuple((jax.ShapeDtypeStruct(shape, dtype...  8.6 us
    ppermute x1, waiting for transfers between devices, per_device(): all_lse = (lse, lax.ppermute(lse, 'cls', [(0, 1), (1, 0)]))  1.11 us
  transfers between devices with their start and end apart: 2, of which 2 were waited for; matrix products, arithmetic and copies ran while one was open for 0% of the time, Pallas kernels for 14%

profile of v3, /device:TPU:0, one launch (start us, length us, event | category | flops | bytes accessed | tf_op | source)
XLA Modules:
  0.0 31.0 jit_solution(16602768287892518591)
XLA Ops:
  0.6 0.0 copy-start
  0.6 1.5 %shard_map.94 = bf16[640,128]{1,0:T(8,128)(2,1)} custom-call(bf16[1,4608]{1,0:T(2,128)(2,1)} %ref_hbm.1), custom_call_target="tpu_custom_call" | custom-call | bytes 163840 | tf_op jit(solution)/shard_map/pallas_call | solution.py:245
  2.1 9.3 %all-to-all-start = ((bf16[16,40,128]{2,1,0:T(8,128)(2,1)}), bf16[16,40,128]{2,1,0:T(8,128)(2,1)S(1)}, u32[]{:S(2)}, u32[]{:S(2)}) async-start(bf16[16,40,128]{2,1,0:T(8,128)(2,1)} %bitcast), calls=%async_computation | async-start | bytes 327680 | tf_op jit(solution)/shard_map/all_to_all | solution.py:291
  11.4 4.2 %shard_map.95 = (bf16[128,4608]{1,0:T(8,128)(2,1)S(1)}, bf16[4608,128]{1,0:T(8,128)(2,1)S(1)}, f32[128,128]{1,0:T(8,128)S(1)}) custom-call(bf16[128,4608]{1,0:T(8,128)(2,1)} %x_hbm.1, s32[2,128]{1,0:T(2,128)} %bitcast.13, s32[1,128]{1,0:T(1,128)} %bitcast.14, f32[1,32]{1,0:T(1,128)} %bitcast.15, f32[40,128]{1,0:T(8,128)} %constant.2.clone.table_hbm), custom_call_target="tpu_custom_call" | custom-call | flops 176947200 | bytes 3538944 | tf_op jit(solution)/shard_map/pallas_call | solution.py:245
  15.6 0.5 %all-to-all-done = bf16[16,40,128]{2,1,0:T(8,128)(2,1)S(1)} async-done(((bf16[16,40,128]{2,1,0:T(8,128)(2,1)}), bf16[16,40,128]{2,1,0:T(8,128)(2,1)S(1)}, u32[]{:S(2)}, u32[]{:S(2)}) %all-to-all-start) | async-done | bytes 163872 | tf_op jit(solution)/shard_map/all_to_all | solution.py:291
  16.1 0.0 copy-done
  16.1 1.1 %shard_map.96 = (f32[288,256]{1,0:T(8,128)S(1)}, f32[1,128]{1,0:T(1,128)S(1)}, f32[1,128]{1,0:T(1,128)S(1)}) custom-call(bf16[640,128]{1,0:T(8,128)(2,1)S(1)} %bitcast.10, bf16[4608,128]{1,0:T(8,128)(2,1)S(1)} %get-tuple-element.13.turned_ref, f32[128,128]{1,0:T(8,128)S(1)} %get-tuple-element.14.power_ref, f32[1,16]{1,0:T(1,128)S(1)} %bitcast.12), custom_call_target="tpu_custom_call" | custom-call | flops 679477248 | bytes 2359296 | tf_op jit(solution)/shard_map/pallas_call | solution.py:245
  17.2 0.1 collective-permute-start
  17.2 1.1 %collective-permute-done.rest_1_ = f32[1,128]{1,0:T(1,128)S(1)} collective-permute-done((f32[1,128]{1,0:T(1,128)S(1)}, f32[1,128]{1,0:T(1,128)S(1)}, u32[]{:S(2)}, u32[]{:S(2)}) %collective-permute-start) | collective-permute-done | bytes 544 | tf_op jit(solution)/shard_map/ppermute | solution.py:317
  18.3 1.2 %shard_map.97 = (bf16[640,128]{1,0:T(8,128)(2,1)S(1)}, f32[1,128]{1,0:T(1,128)}) custom-call(f32[288,256]{1,0:T(8,128)S(1)} %get-tuple-element.15.e_ref, f32[1,128]{1,0:T(1,128)S(1)} %get-tuple-element.16.best_ref, bf16[128,4608]{1,0:T(8,128)(2,1)S(1)} %get-tuple-element.17.adj_ref, f32[128,128]{1,0:T(8,128)S(1)} %get-tuple-element.14.power_ref, ...), custom_call_target="tpu_custom_call" | custom-call | flops 679477248 | bytes 2359296 | tf_op jit(solution)/shard_map/pallas_call | solution.py:245
  19.6 10.8 %all_to_all.22 = bf16[16,40,128]{2,1,0:T(8,128)(2,1)S(1)} all-to-all(bf16[16,40,128]{2,1,0:T(8,128)(2,1)S(1)} %bitcast.11), channel_id=1, replica_groups={{22,24,26,28,30,0,2,4,6,8,10,12,14,16,18,20},{23,25,27,29,31,1,3,5,7,9,..., dimensions={0} | all-to-all | bytes 327680 | tf_op jit(solution)/shard_map/all_to_all | solution.py:327
  30.4 0.6 %shard_map.98 = (f32[1,4608]{1,0:T(1,128)}, f32[1,32]{1,0:T(1,128)}) custom-call(bf16[640,128]{1,0:T(8,128)(2,1)S(1)} %bitcast.9), custom_call_target="tpu_custom_call" | custom-call | bytes 163840 | tf_op jit(solution)/shard_map/pallas_call | solution.py:245
Async XLA Ops:
  0.6 15.5 %copy-start = (f32[16]{0:T(128)S(1)}, f32[16]{0:T(128)}, u32[]{:S(2)}) copy-start(f32[16]{0:T(128)} %param.9) | copy-start | bytes 196
  2.1 14.0 %all-to-all-start = ((bf16[16,40,128]{2,1,0:T(8,128)(2,1)}), bf16[16,40,128]{2,1,0:T(8,128)(2,1)S(1)}, u32[]{:S(2)}, u32[]{:S(2)}) async-start(bf16[16,40,128]{2,1,0:T(8,128)(2,1)} %bitcast), calls=%async_computation | async-start | bytes 327680 | tf_op jit(solution)/shard_map/all_to_all | solution.py:291
  17.2 1.2 %collective-permute-start = (f32[1,128]{1,0:T(1,128)S(1)}, f32[1,128]{1,0:T(1,128)S(1)}, u32[]{:S(2)}, u32[]{:S(2)}) collective-permute-start(f32[1,128]{1,0:T(1,128)S(1)} %get-tuple-element.18.rest_0_), channel_id=1, source_target_pairs={{0,1},{1,0},{2,3},{3,2},{4,5},{5,4},{6,7},{7,6},{8,9},{9,8},{10,11... | collective-permute-start | bytes 1544 | tf_op jit(solution)/shard_map/ppermute | solution.py:317

commit v4 on v2

--- a/solution.py
+++ b/solution.py
@@ -17,6 +17,7 @@
 HALF = ROT // 2
 GROUP = 3
 CHUNK = 40
+ORDER = [11, 10, 0, 5, 6, 4, 14, 1, 15, 8, 13, 7, 3, 2, 12, 9]
 F32 = jnp.float32
 BF16 = jnp.bfloat16
 HIGHEST = lax.Precision.HIGHEST
@@ -64,17 +65,15 @@
     return np.stack(rows).astype(np.float32)
 
 
-def spread_kernel(copies, ref_ref, out_ref, rows):
+def retile_kernel(ref_ref, out_ref, rows):
     owned = ref_ref.shape[0]
     blocks = ref_ref.shape[1] // LANES
     for o in range(owned):
         row = ref_ref[o : o + 1, :].astype(F32)
-        base = o * CHUNK
         for j in range(blocks):
-            rows[base + j : base + j + 1, :] = row[:, j * LANES : (j + 1) * LANES]
-        rows[base + blocks : base + CHUNK, :] = jnp.zeros((CHUNK - blocks, LANES), F32)
-    one = rows[...]
-    out_ref[...] = jnp.concatenate([one] * copies, axis=0).astype(BF16)
+            rows[o * CHUNK + j : o * CHUNK + j + 1, :] = row[:, j * LANES : (j + 1) * LANES]
+        rows[o * CHUNK + blocks : (o + 1) * CHUNK, :] = jnp.zeros((CHUNK - blocks, LANES), F32)
+    out_ref[...] = rows[...].astype(BF16)
 
 
 def prepare_kernel(
@@ -137,12 +136,14 @@
             turned_ref[tile * LANES : (tile + 1) * LANES, :] = out.T.astype(BF16)
 
 
-def score_kernel(got_ref, turned_ref, power_ref, prior_ref, e_ref, best_ref, lse_ref, wide):
+def score_kernel(held, got_ref, turned_ref, power_ref, prior_ref, e_ref, best_ref, lse_ref, wide):
     classes = prior_ref.shape[1]
     particles = turned_ref.shape[1]
-    diagonal = lax.broadcasted_iota(jnp.int32, (classes, classes), 0) == lax.broadcasted_iota(
-        jnp.int32, (classes, classes), 1
-    )
+    row = lax.broadcasted_iota(jnp.int32, (classes, classes), 0)
+    place = jnp.zeros((classes, classes), jnp.int32)
+    for i, c in enumerate(held):
+        place = jnp.where(row == i, c, place)
+    diagonal = place == lax.broadcasted_iota(jnp.int32, (classes, classes), 1)
     prior = jnp.sum(jnp.where(diagonal, jnp.broadcast_to(prior_ref[...], (classes, classes)), 0.0), axis=1, keepdims=True)
     wide[...] = got_ref[...].astype(F32)
     blocks = []
@@ -174,15 +175,17 @@
     lse_ref[...] = best + jnp.log(total)
 
 
+def total_evidence(lse_refs):
+    lse = jnp.concatenate([ref[...] for ref in lse_refs], axis=0)
+    top = jnp.max(lse, axis=0, keepdims=True)
+    return top + jnp.log(jnp.sum(jnp.exp(lse - top), axis=0, keepdims=True))
+
+
 def sum_kernel(e_ref, best_ref, adj_ref, power_ref, *rest):
-    *lse_refs, out_ref, evidence_ref, wide = rest
+    *lse_refs, out_ref, wide = rest
     particles = adj_ref.shape[0]
     classes = e_ref.shape[0] // HALF
-    lse = jnp.concatenate([ref[...] for ref in lse_refs], axis=0)
-    top = jnp.max(lse, axis=0, keepdims=True)
-    evidence = top + jnp.log(jnp.sum(jnp.exp(lse - top), axis=0, keepdims=True))
-    evidence_ref[...] = evidence
-    factor = jnp.exp(best_ref[...] - evidence)
+    factor = jnp.exp(best_ref[...] - total_evidence(lse_refs))
     post = e_ref[...] * jnp.concatenate([factor, factor], axis=1)
     mass = jnp.sum(post.reshape(HALF, classes, 2 * particles), axis=0)
     mass = mass[:, :particles] + mass[:, particles:]
@@ -214,7 +217,9 @@
     out_ref[...] = wide[...].astype(BF16)
 
 
-def final_kernel(senders, got_ref, data_ref, weight_ref):
+def final_kernel(senders, got_ref, *rest):
+    *lse_refs, data_ref, weight_ref, evidence_ref = rest
+    evidence_ref[...] = total_evidence(lse_refs)
     owned = data_ref.shape[0]
     got = got_ref[...].astype(F32).reshape(senders, owned * CHUNK, LANES)
     total = jnp.sum(got, axis=0)
@@ -228,20 +233,27 @@
         )
 
 
-def call(kernel, outs, scratch=(), in_hbm=(), flops=0, bytes_accessed=0):
+def call(kernel, outs, scratch=(), in_hbm=(), out_space=pltpu.VMEM, flops=0, bytes_accessed=0):
     def run(*args):
         args = [pltpu.with_memory_space_constraint(x, pltpu.HBM) if i in in_hbm else x for i, x in enumerate(args)]
         return pl.pallas_call(
             kernel,
             out_shape=tuple(jax.ShapeDtypeStruct(shape, dtype) for shape, dtype in outs),
             in_specs=[pl.BlockSpec(memory_space=pltpu.HBM if i in in_hbm else pltpu.VMEM) for i in range(len(args))],
-            out_specs=tuple(pl.BlockSpec(memory_space=pltpu.VMEM) for _ in outs),
+            out_specs=tuple(pl.BlockSpec(memory_space=out_space) for _ in outs),
             scratch_shapes=list(scratch),
             compiler_params=pltpu.CompilerParams(vmem_limit_bytes=VMEM_LIMIT),
             cost_estimate=pl.CostEstimate(flops=flops, bytes_accessed=bytes_accessed, transcendentals=0),
         )(*args)
 
     return run
+
+
+def exchange_order(dom_size):
+    if dom_size == len(ORDER):
+        return ORDER
+    root = dom_size * 3 // 4 - 1
+    return [(i + root) % dom_size for i in range(dom_size)]
 
 
 def per_device(particles, references, log_prior, noise_var, offsets, groups):
@@ -253,13 +265,23 @@
     message = classes * CHUNK
     table = lane_tables()
 
-    (spread,) = call(
-        functools.partial(spread_kernel, dom_size),
-        [((message, LANES), BF16)],
+    order = exchange_order(dom_size)
+    exchange = functools.partial(
+        lax.all_to_all,
+        axis_name="dom",
+        split_axis=0,
+        concat_axis=0,
+        axis_index_groups=[order],
+        tiled=True,
+    )
+    (own,) = call(
+        retile_kernel,
+        [((owned * CHUNK, LANES), BF16)],
         [pltpu.VMEM((owned * CHUNK, LANES), F32)],
         bytes_accessed=message * LANES * 2,
     )(references)
-    got = lax.all_to_all(spread, "dom", 0, 0, tiled=True)
+    spread = jnp.broadcast_to(own[None], (dom_size, owned * CHUNK, LANES)).reshape(message, LANES)
+    got = exchange(spread)
     adjusted, turned, power = call(
         prepare_kernel,
         [((rows, samples), BF16), ((samples, rows), BF16), ((rows, LANES), F32)],
@@ -278,7 +300,7 @@
     )(particles, offsets.T, groups.reshape(1, rows), noise_var.reshape(1, CYCLES), jnp.asarray(table))
     dot_flops = 2 * ROT * classes * rows * samples
     e, best, lse = call(
-        score_kernel,
+        functools.partial(score_kernel, [d * owned + o for d in order for o in range(owned)]),
         [((HALF * classes, 2 * rows), F32), ((1, rows), F32), ((1, rows), F32)],
         [pltpu.VMEM((message, LANES), F32)],
         flops=dot_flops,
@@ -288,19 +310,19 @@
         all_lse = (lse, lax.ppermute(lse, "cls", [(0, 1), (1, 0)]))
     else:
         all_lse = (lax.all_gather(lse, "cls", axis=0, tiled=True),)
-    sums, evidence = call(
+    (sums,) = call(
         sum_kernel,
-        [((message, LANES), BF16), ((1, rows), F32)],
+        [((message, LANES), BF16)],
         [pltpu.VMEM((message, LANES), F32)],
         flops=dot_flops,
         bytes_accessed=rows * samples * 4,
     )(e, best, adjusted, power, *all_lse)
-    mine = lax.all_to_all(sums, "dom", 0, 0, tiled=True)
-    data, weight = call(
+    mine = exchange(sums)
+    data, weight, evidence = call(
         functools.partial(final_kernel, dom_size),
-        [((owned, samples), F32), ((owned, CYCLES), F32)],
+        [((owned, samples), F32), ((owned, CYCLES), F32), ((1, rows), F32)],
         bytes_accessed=message * LANES * 2,
-    )(mine)
+    )(mine, *all_lse)
     return data, weight, evidence.reshape(rows)
 
 

time: 34.1 us -> 30.4 us (0.89)
  waiting for transfers between devices: 4.83 us -> 1.11 us
  starting transfers between devices: 8.38 us -> 9.3 us
  Pallas kernels: 7.8 us -> 6.91 us
  blocking collectives: 11.4 us -> 10.6 us
  local copies, waits for them, and re-layouts: 0.72 us -> 1.4 us
    all_to_all x1, waiting for transfers between devices: 3.72 us -> 0.01 us  [per_device(): got = exchange(spread)]
    all_to_all x1, starting transfers between devices: 8.31 us -> 9.23 us  [per_device(): got = exchange(spread)]
    pallas_call x5, Pallas kernels: 7.8 us -> 6.91 us  [run(): pl.pallas_call(kernel, out_shape=tuple((jax.ShapeDtypeStruct(shape, dtype...]
    all_to_all x1, blocking collectives: 11.4 us -> 10.6 us  [per_device(): mine = exchange(sums)]
    broadcast_in_dim x0 -> x1, local copies, waits for them, and re-layouts: none -> 0.68 us  [per_device(): jnp.broadcast_to(own[None], (dom_size, owned * CHUNK, LANES))]
  transfers between devices with their start and end apart: 2 -> 2, of which waited for: 2 -> 1; matrix products, arithmetic and copies ran while one was open for 0% -> 0% of each run, Pallas kernels for 12% -> 14%
where the time goes in v4:
time: 30.4 us; the launch traced here: 30 us
  blocking collectives  10.6 us (35%)
  starting transfers between devices  9.3 us (31%)
  Pallas kernels  6.91 us (23%)
  local copies, waits for them, and re-layouts  1.4 us (5%)
  waiting for transfers between devices  1.11 us (4%)
  between operations  0.68 us (2%)
    all_to_all x1, blocking collectives, per_device(): mine = exchange(sums)  10.6 us
    all_to_all x1, starting transfers between devices, per_device(): got = exchange(spread)  9.23 us
    pallas_call x5, Pallas kernels, run(): pl.pallas_call(kernel, out_shape=tuple((jax.ShapeDtypeStruct(shape, dtype...  6.91 us
    ppermute x1, waiting for transfers between devices, per_device(): all_lse = (lse, lax.ppermute(lse, 'cls', [(0, 1), (1, 0)]))  1.11 us
    unnamed x4, local copies, waits for them, and re-layouts  0.72 us
    broadcast_in_dim x1, local copies, waits for them, and re-layouts, per_device(): jnp.broadcast_to(own[None], (dom_size, owned * CHUNK, LANES))  0.68 us
  transfers between devices with their start and end apart: 2, of which 1 were waited for; matrix products, arithmetic and copies ran while one was open for 0% of the time, Pallas kernels for 14%

profile of v4, /device:TPU:0, one launch (start us, length us, event | category | flops | bytes accessed | tf_op | source)
XLA Modules:
  0.0 30.0 jit_solution(6067717059753188153)
XLA Ops:
  0.6 0.0 copy-start
  0.6 0.7 %copy-done = bf16[1,4608]{1,0:T(2,128)(2,1)S(1)} copy-done((bf16[1,4608]{1,0:T(2,128)(2,1)S(1)}, bf16[1,4608]{1,0:T(2,128)(2,1)}, u32[]{:S(2)}) %copy-start) | copy-done | bytes 9240
  1.4 0.0 copy-start.1
  1.4 0.7 %broadcast_in_dim.2 = bf16[16,40,128]{2,1,0:T(8,128)(2,1)} broadcast(bf16[40,128]{1,0:T(8,128)(2,1)S(1)} %shard_map.94), dimensions={1,2} | broadcast | bytes 174080 | tf_op jit(solution)/shard_map/broadcast_in_dim | solution.py:283
  2.1 9.2 %all-to-all-start = ((bf16[16,40,128]{2,1,0:T(8,128)(2,1)}), bf16[16,40,128]{2,1,0:T(8,128)(2,1)S(1)}, u32[]{:S(2)}, u32[]{:S(2)}) async-start(bf16[16,40,128]{2,1,0:T(8,128)(2,1)} %broadcast_in_dim.2), calls=%async_computation | async-start | bytes 327680 | tf_op jit(solution)/shard_map/all_to_all | solution.py:284
  11.3 4.2 %shard_map.95 = (bf16[128,4608]{1,0:T(8,128)(2,1)S(1)}, bf16[4608,128]{1,0:T(8,128)(2,1)S(1)}, f32[128,128]{1,0:T(8,128)S(1)}) custom-call(bf16[128,4608]{1,0:T(8,128)(2,1)} %x_hbm.1, s32[2,128]{1,0:T(2,128)} %bitcast.12, s32[1,128]{1,0:T(1,128)} %bitcast.13, f32[1,32]{1,0:T(1,128)} %bitcast.14, f32[40,128]{1,0:T(8,128)} %constant.2.clone.table_hbm), custom_call_target="tpu_custom_call" | custom-call | flops 176947200 | bytes 3538944 | tf_op jit(solution)/shard_map/pallas_call | solution.py:239
  15.5 0.0 all-to-all-done
  15.5 0.0 copy-done.1
  15.5 1.1 %shard_map.96 = (f32[288,256]{1,0:T(8,128)S(1)}, f32[1,128]{1,0:T(1,128)S(1)}, f32[1,128]{1,0:T(1,128)S(1)}) custom-call(bf16[640,128]{1,0:T(8,128)(2,1)S(1)} %bitcast.9, bf16[4608,128]{1,0:T(8,128)(2,1)S(1)} %get-tuple-element.12.turned_ref, f32[128,128]{1,0:T(8,128)S(1)} %get-tuple-element.13.power_ref, f32[1,16]{1,0:T(1,128)S(1)} %bitcast.11), custom_call_target="tpu_custom_call" | custom-call | flops 679477248 | bytes 2359296 | tf_op jit(solution)/shard_map/pallas_call | solution.py:239
  16.6 0.1 collective-permute-start
  16.7 1.1 %collective-permute-done.rest_1_ = f32[1,128]{1,0:T(1,128)S(1)} collective-permute-done((f32[1,128]{1,0:T(1,128)S(1)}, f32[1,128]{1,0:T(1,128)S(1)}, u32[]{:S(2)}, u32[]{:S(2)}) %collective-permute-start) | collective-permute-done | bytes 544 | tf_op jit(solution)/shard_map/ppermute | solution.py:310
  17.8 1.0 %shard_map.97 = bf16[640,128]{1,0:T(8,128)(2,1)S(1)} custom-call(f32[288,256]{1,0:T(8,128)S(1)} %get-tuple-element.14.e_ref, f32[1,128]{1,0:T(1,128)S(1)} %get-tuple-element.15.best_ref, bf16[128,4608]{1,0:T(8,128)(2,1)S(1)} %get-tuple-element.16.adj_ref, f32[128,128]{1,0:T(8,128)S(1)} %get-tuple-element.13.power_ref, ...), custom_call_target="tpu_custom_call" | custom-call | flops 679477248 | bytes 2359296 | tf_op jit(solution)/shard_map/pallas_call | solution.py:239
  18.8 10.6 %all_to_all.19 = bf16[16,40,128]{2,1,0:T(8,128)(2,1)S(1)} all-to-all(bf16[16,40,128]{2,1,0:T(8,128)(2,1)S(1)} %bitcast.10), channel_id=1, replica_groups={{22,20,0,10,12,8,28,2,30,16,26,14,6,4,24,18},{23,21,1,11,13,9,29,3,31,1..., dimensions={0} | all-to-all | bytes 327680 | tf_op jit(solution)/shard_map/all_to_all | solution.py:320
  29.4 0.6 %shard_map.98 = (f32[1,4608]{1,0:T(1,128)}, f32[1,32]{1,0:T(1,128)}, f32[1,128]{1,0:T(1,128)}) custom-call(bf16[640,128]{1,0:T(8,128)(2,1)S(1)} %bitcast.8, f32[1,128]{1,0:T(1,128)S(1)} %get-tuple-element.17.rest_0_, f32[1,128]{1,0:T(1,128)S(1)} %collective-permute-done.rest_1_), custom_call_target="tpu_custom_call" | custom-call | bytes 163840 | tf_op jit(solution)/shard_map/pallas_call | solution.py:239
  (1 shorter events, 0.0 us)
Async XLA Ops:
  0.6 0.7 %copy-start = (bf16[1,4608]{1,0:T(2,128)(2,1)S(1)}, bf16[1,4608]{1,0:T(2,128)(2,1)}, u32[]{:S(2)}) copy-start(bf16[1,4608]{1,0:T(2,128)(2,1)} %ref_ref.1) | copy-start | bytes 27652
  1.4 14.2 %copy-start.1 = (f32[16]{0:T(128)S(1)}, f32[16]{0:T(128)}, u32[]{:S(2)}) copy-start(f32[16]{0:T(128)} %param.9) | copy-start | bytes 196
  2.1 13.4 %all-to-all-start = ((bf16[16,40,128]{2,1,0:T(8,128)(2,1)}), bf16[16,40,128]{2,1,0:T(8,128)(2,1)S(1)}, u32[]{:S(2)}, u32[]{:S(2)}) async-start(bf16[16,40,128]{2,1,0:T(8,128)(2,1)} %broadcast_in_dim.2), calls=%async_computation | async-start | bytes 327680 | tf_op jit(solution)/shard_map/all_to_all | solution.py:284
  16.6 1.2 %collective-permute-start = (f32[1,128]{1,0:T(1,128)S(1)}, f32[1,128]{1,0:T(1,128)S(1)}, u32[]{:S(2)}, u32[]{:S(2)}) collective-permute-start(f32[1,128]{1,0:T(1,128)S(1)} %get-tuple-element.17.rest_0_), channel_id=1, source_target_pairs={{0,1},{1,0},{2,3},{3,2},{4,5},{5,4},{6,7},{7,6},{8,9},{9,8},{10,11... | collective-permute-start | bytes 1544 | tf_op jit(solution)/shard_map/ppermute | solution.py:310

commit v5 on v4

--- a/solution.py
+++ b/solution.py
@@ -15,7 +15,8 @@
 ANGLES = 72
 LANES = 128
 HALF = ROT // 2
-GROUP = 3
+PARTS = 4
+AHEAD = 6
 CHUNK = 40
 ORDER = [11, 10, 0, 5, 6, 4, 14, 1, 15, 8, 13, 7, 3, 2, 12, 9]
 F32 = jnp.float32
@@ -28,7 +29,7 @@
     nodes = 0.125 + 0.125 * np.cos(np.pi * (np.arange(400) + 0.5) / 400)
     root = np.sqrt(nodes)
     fits = []
-    for values, degree in ((np.cos(2 * np.pi * root), 7), (np.sin(2 * np.pi * root) / root, 7)):
+    for values, degree in ((np.cos(2 * np.pi * root), 6), (np.sin(2 * np.pi * root) / root, 5)):
         fit = np.polynomial.Chebyshev.fit(nodes, values, degree, domain=[0, 0.25])
         fits.append([float(c) for c in fit.convert(kind=np.polynomial.Polynomial).coef])
     return fits
@@ -78,10 +79,9 @@
 
 def prepare_kernel(
     x_hbm, off_hbm, grp_hbm, noise_hbm, table_hbm, adj_ref, turned_ref, power_ref, x_ref, off_ref, grp_ref, noise_ref,
-    table_ref, small_sems, x_sems
+    table_ref, cos_ref, sin_ref, small_sems, x_sems
 ):
     rows = x_ref.shape[0]
-    width = GROUP * LANES
     small = [
         pltpu.make_async_copy(source, target, small_sems.at[i])
         for i, (source, target) in enumerate(
@@ -91,9 +91,10 @@
     for copy in small:
         copy.start()
     parts = []
-    for g in range(2 * HALF // GROUP):
-        part = slice((g // 2 + g % 2 * (HALF // GROUP)) * width, (g // 2 + g % 2 * (HALF // GROUP) + 1) * width)
-        copy = pltpu.make_async_copy(x_hbm.at[:, part], x_ref.at[:, part], x_sems.at[g])
+    step = rows // PARTS
+    for g in range(PARTS):
+        part = slice(g * step, (g + 1) * step)
+        copy = pltpu.make_async_copy(x_hbm.at[part, :], x_ref.at[part, :], x_sems.at[g])
         copy.start()
         parts.append(copy)
     out_lane = lax.broadcasted_iota(jnp.int32, (LANES, LANES), 1)
@@ -118,14 +119,18 @@
     power_ref[...] = ctf * scale
     shift_x = down(off_ref[0:1, :])
     shift_y = down(off_ref[1:2, :])
-    for t in range(HALF):
-        if t % GROUP == 0:
-            for copy in parts[2 * (t // GROUP) : 2 * (t // GROUP) + 2]:
-                copy.wait()
+
+    def phases(t):
         turns = shift_x * table_ref[t : t + 1, :] + shift_y * table_ref[HALF + t : HALF + t + 1, :]
         cosine, sine = turn_trig(turns)
-        cosine = cosine * scale
-        sine = sine * scale
+        return cosine * scale, sine * scale
+
+    for t in range(AHEAD):
+        cos_ref[t], sin_ref[t] = phases(t)
+    for copy in parts:
+        copy.wait()
+    for t in range(HALF):
+        cosine, sine = (cos_ref[t], sin_ref[t]) if t < AHEAD else phases(t)
         for tile, sign in ((t, 1), (t + HALF, -1)):
             x = x_ref[:, tile * LANES : (tile + 1) * LANES]
             other = jnp.dot(x, swap, preferred_element_type=F32)
@@ -136,7 +141,7 @@
             turned_ref[tile * LANES : (tile + 1) * LANES, :] = out.T.astype(BF16)
 
 
-def score_kernel(held, got_ref, turned_ref, power_ref, prior_ref, e_ref, best_ref, lse_ref, wide):
+def score(held, got_ref, turned_ref, power_ref, prior_ref, e_ref, best_ref, lse_ref, wide):
     classes = prior_ref.shape[1]
     particles = turned_ref.shape[1]
     row = lax.broadcasted_iota(jnp.int32, (classes, classes), 0)
@@ -175,13 +180,40 @@
     lse_ref[...] = best + jnp.log(total)
 
 
+def first_score_kernel(held, alone, *refs):
+    *rest, lse_ref, _ = refs
+    here = True if alone else lax.axis_index("cls") == 1
+
+    @pl.when(here)
+    def _():
+        score(held, *refs)
+
+    @pl.when(jnp.logical_not(here))
+    def _():
+        lse_ref[...] = jnp.zeros_like(lse_ref)
+
+
+def second_score_kernel(held, *refs):
+    sources, before, after, wide = refs[:4], refs[4:7], refs[7:10], refs[10]
+    here = lax.axis_index("cls") == 0
+
+    @pl.when(here)
+    def _():
+        score(held, *sources, *after, wide)
+
+    @pl.when(jnp.logical_not(here))
+    def _():
+        for source, target in zip(before, after):
+            target[...] = source[...]
+
+
 def total_evidence(lse_refs):
     lse = jnp.concatenate([ref[...] for ref in lse_refs], axis=0)
     top = jnp.max(lse, axis=0, keepdims=True)
     return top + jnp.log(jnp.sum(jnp.exp(lse - top), axis=0, keepdims=True))
 
 
-def sum_kernel(e_ref, best_ref, adj_ref, power_ref, *rest):
+def sums(e_ref, best_ref, adj_ref, power_ref, *rest):
     *lse_refs, out_ref, wide = rest
     particles = adj_ref.shape[0]
     classes = e_ref.shape[0] // HALF
@@ -215,6 +247,25 @@
     for n in range(ROT + 1, CHUNK):
         wide[pl.ds(n, classes, stride=CHUNK), :] = jnp.zeros((classes, LANES), F32)
     out_ref[...] = wide[...].astype(BF16)
+
+
+def first_sum_kernel(alone, *refs):
+    @pl.when(True if alone else lax.axis_index("cls") == 0)
+    def _():
+        sums(*refs)
+
+
+def second_sum_kernel(*refs):
+    *sources, before, out_ref, wide = refs
+    here = lax.axis_index("cls") == 1
+
+    @pl.when(here)
+    def _():
+        sums(*sources, out_ref, wide)
+
+    @pl.when(jnp.logical_not(here))
+    def _():
+        out_ref[...] = before[...]
 
 
 def final_kernel(senders, got_ref, *rest):
@@ -291,33 +342,42 @@
             pltpu.VMEM((1, rows), jnp.int32),
             pltpu.VMEM((1, CYCLES), F32),
             pltpu.VMEM(table.shape, F32),
+            pltpu.VMEM((AHEAD, rows, LANES), F32),
+            pltpu.VMEM((AHEAD, rows, LANES), F32),
             pltpu.SemaphoreType.DMA((4,)),
-            pltpu.SemaphoreType.DMA((2 * HALF // GROUP,)),
+            pltpu.SemaphoreType.DMA((PARTS,)),
         ],
         in_hbm=range(5),
         flops=rows * samples * 300,
         bytes_accessed=rows * samples * 6,
     )(particles, offsets.T, groups.reshape(1, rows), noise_var.reshape(1, CYCLES), jnp.asarray(table))
     dot_flops = 2 * ROT * classes * rows * samples
-    e, best, lse = call(
-        functools.partial(score_kernel, [d * owned + o for d in order for o in range(owned)]),
-        [((HALF * classes, 2 * rows), F32), ((1, rows), F32), ((1, rows), F32)],
-        [pltpu.VMEM((message, LANES), F32)],
-        flops=dot_flops,
-        bytes_accessed=rows * samples * 4,
-    )(got, turned, power, log_prior.reshape(1, classes))
-    if cls_size == 2:
+    held = [d * owned + o for d in order for o in range(owned)]
+    prior = log_prior.reshape(1, classes)
+    scored = [((HALF * classes, 2 * rows), F32), ((1, rows), F32), ((1, rows), F32)]
+    wide = [pltpu.VMEM((message, LANES), F32)]
+    costs = dict(flops=dot_flops, bytes_accessed=rows * samples * 4)
+    summed = [((message, LANES), BF16)]
+    two = cls_size == 2
+    e, best, lse = call(functools.partial(first_score_kernel, held, not two), scored, wide, **costs)(
+        got, turned, power, prior
+    )
+    if two:
+        early = lax.ppermute(lse, "cls", [(0, 1), (1, 0)])
+        e, best, lse = call(functools.partial(second_score_kernel, held), scored, wide, **costs)(
+            got, turned, power, prior, e, best, lse
+        )
         all_lse = (lse, lax.ppermute(lse, "cls", [(0, 1), (1, 0)]))
+        (part,) = call(functools.partial(first_sum_kernel, False), summed, wide, **costs)(
+            e, best, adjusted, power, lse, early
+        )
+        (partial_sums,) = call(second_sum_kernel, summed, wide, **costs)(e, best, adjusted, power, *all_lse, part)
     else:
         all_lse = (lax.all_gather(lse, "cls", axis=0, tiled=True),)
-    (sums,) = call(
-        sum_kernel,
-        [((message, LANES), BF16)],
-        [pltpu.VMEM((message, LANES), F32)],
-        flops=dot_flops,
-        bytes_accessed=rows * samples * 4,
-    )(e, best, adjusted, power, *all_lse)
-    mine = exchange(sums)
+        (partial_sums,) = call(functools.partial(first_sum_kernel, True), summed, wide, **costs)(
+            e, best, adjusted, power, *all_lse
+        )
+    mine = exchange(partial_sums)
     data, weight, evidence = call(
         functools.partial(final_kernel, dom_size),
         [((owned, samples), F32), ((owned, CYCLES), F32), ((1, rows), F32)],

time: 30.4 us -> 29.5 us (0.970)
  Pallas kernels: 6.91 us -> 6.11 us
    ppermute x1, waiting for transfers between devices: 1.11 us -> 0.11 us  [per_device(): all_lse = (lse, lax.ppermute(lse, 'cls', [(0, 1), (1, 0)]))]
    all_to_all x1, waiting for transfers between devices: 0.01 us -> 0.83 us  [per_device(): got = exchange(spread)]
    pallas_call x5 -> x7, Pallas kernels: 6.91 us -> 6.11 us  [run(): pl.pallas_call(kernel, out_shape=tuple((jax.ShapeDtypeStruct(shape, dtype...]
  transfers between devices with their start and end apart: 2 -> 3, of which waited for: 1 -> 2; matrix products, arithmetic and copies ran while one was open for 0% -> 0% of each run, Pallas kernels for 14% -> 19%
where the time goes in v5:
time: 29.5 us; the launch traced here: 29.2 us
  blocking collectives  10.8 us (37%)
  starting transfers between devices  9.3 us (32%)
  Pallas kernels  6.11 us (21%)
  local copies, waits for them, and re-layouts  1.4 us (5%)
  waiting for transfers between devices  0.94 us (3%)
  between operations  0.69 us (2%)
    all_to_all x1, blocking collectives, per_device(): mine = exchange(partial_sums)  10.8 us
    all_to_all x1, starting transfers between devices, per_device(): got = exchange(spread)  9.23 us
    pallas_call x7, Pallas kernels, run(): pl.pallas_call(kernel, out_shape=tuple((jax.ShapeDtypeStruct(shape, dtype...  6.11 us
    all_to_all x1, waiting for transfers between devices, per_device(): got = exchange(spread)  0.83 us
    unnamed x4, local copies, waits for them, and re-layouts  0.72 us
    broadcast_in_dim x1, local copies, waits for them, and re-layouts, per_device(): jnp.broadcast_to(own[None], (dom_size, owned * CHUNK, LANES))  0.68 us
  transfers between devices with their start and end apart: 3, of which 2 were waited for; matrix products, arithmetic and copies ran while one was open for 0% of the time, Pallas kernels for 19%

profile of v5, /device:TPU:0, one launch (start us, length us, event | category | flops | bytes accessed | tf_op | source)
XLA Modules:
  0.0 29.2 jit_solution(403415396471684951)
XLA Ops:
  0.6 0.0 copy-start
  0.6 0.7 %copy-done = bf16[1,4608]{1,0:T(2,128)(2,1)S(1)} copy-done((bf16[1,4608]{1,0:T(2,128)(2,1)S(1)}, bf16[1,4608]{1,0:T(2,128)(2,1)}, u32[]{:S(2)}) %copy-start) | copy-done | bytes 9240
  1.4 0.0 copy-start.1
  1.4 0.7 %broadcast_in_dim.2 = bf16[16,40,128]{2,1,0:T(8,128)(2,1)} broadcast(bf16[40,128]{1,0:T(8,128)(2,1)S(1)} %shard_map.94), dimensions={1,2} | broadcast | bytes 174080 | tf_op jit(solution)/shard_map/broadcast_in_dim | solution.py:334
  2.1 9.2 %all-to-all-start = ((bf16[16,40,128]{2,1,0:T(8,128)(2,1)}), bf16[16,40,128]{2,1,0:T(8,128)(2,1)S(1)}, u32[]{:S(2)}, u32[]{:S(2)}) async-start(bf16[16,40,128]{2,1,0:T(8,128)(2,1)} %broadcast_in_dim.2), calls=%async_computation | async-start | bytes 327680 | tf_op jit(solution)/shard_map/all_to_all | solution.py:335
  11.3 3.4 %shard_map.95 = (bf16[128,4608]{1,0:T(8,128)(2,1)S(1)}, bf16[4608,128]{1,0:T(8,128)(2,1)S(1)}, f32[128,128]{1,0:T(8,128)S(1)}) custom-call(bf16[128,4608]{1,0:T(8,128)(2,1)} %x_hbm.1, s32[2,128]{1,0:T(2,128)} %bitcast.14, s32[1,128]{1,0:T(1,128)} %bitcast.15, f32[1,32]{1,0:T(1,128)} %bitcast.16, f32[40,128]{1,0:T(8,128)} %constant.2.clone.table_hbm), custom_call_target="tpu_custom_call" | custom-call | flops 176947200 | bytes 3538944 | tf_op jit(solution)/shard_map/pallas_call | solution.py:290
  14.7 0.8 %all-to-all-done = bf16[16,40,128]{2,1,0:T(8,128)(2,1)S(1)} async-done(((bf16[16,40,128]{2,1,0:T(8,128)(2,1)}), bf16[16,40,128]{2,1,0:T(8,128)(2,1)S(1)}, u32[]{:S(2)}, u32[]{:S(2)}) %all-to-all-start) | async-done | bytes 163872 | tf_op jit(solution)/shard_map/all_to_all | solution.py:335
  15.5 0.0 copy-done.1
  15.5 0.0 collective-permute-start.1
  15.5 1.1 %shard_map.97 = (f32[288,256]{1,0:T(8,128)S(1)}, f32[1,128]{1,0:T(1,128)S(1)}, f32[1,128]{1,0:T(1,128)S(1)}) custom-call(bf16[640,128]{1,0:T(8,128)(2,1)S(1)} %bitcast.10, bf16[4608,128]{1,0:T(8,128)(2,1)S(1)} %get-tuple-element.15.refs_1_, f32[128,128]{1,0:T(8,128)S(1)} %get-tuple-element.16.refs_2_.refs_3_, f32[1,16]{1,0:T(1,128)S(1)} %bitcast.13, ...), custom_call_target="tpu_custom_call" | custom-call | flops 679477248 | bytes 2359296 | tf_op jit(solution)/shard_map/pallas_call | solution.py:290
  16.6 0.1 collective-permute-start
  16.7 0.0 collective-permute-done.1.refs_5_
  16.7 1.0 %shard_map.98.refs_6_ = bf16[640,128]{1,0:T(8,128)(2,1)S(1)} custom-call(f32[288,256]{1,0:T(8,128)S(1)} %get-tuple-element.20.refs_0_, f32[1,128]{1,0:T(1,128)S(1)} %get-tuple-element.21.refs_1_, bf16[128,4608]{1,0:T(8,128)(2,1)S(1)} %get-tuple-element.22.refs_2_, f32[128,128]{1,0:T(8,128)S(1)} %get-tuple-element.16.refs_2_.refs_3_, ...), custom_call_target="tpu_custom_call" | custom-call | flops 679477248 | bytes 2359296 | tf_op jit(solution)/shard_map/pallas_call | solution.py:290
  17.7 0.1 collective-permute-done.refs_5_.rest_1_
  17.8 10.8 %all_to_all.19 = bf16[16,40,128]{2,1,0:T(8,128)(2,1)S(1)} all-to-all(bf16[16,40,128]{2,1,0:T(8,128)(2,1)S(1)} %bitcast.11), channel_id=1, replica_groups={{22,20,0,10,12,8,28,2,30,16,26,14,6,4,24,18},{23,21,1,11,13,9,29,3,31,1..., dimensions={0} | all-to-all | bytes 327680 | tf_op jit(solution)/shard_map/all_to_all | solution.py:380
  28.6 0.6 %shard_map.100 = (f32[1,4608]{1,0:T(1,128)}, f32[1,32]{1,0:T(1,128)}, f32[1,128]{1,0:T(1,128)}) custom-call(bf16[640,128]{1,0:T(8,128)(2,1)S(1)} %bitcast.8, f32[1,128]{1,0:T(1,128)S(1)} %get-tuple-element.23.refs_4_.rest_0_, f32[1,128]{1,0:T(1,128)S(1)} %collective-permute-done.refs_5_.rest_1_), custom_call_target="tpu_custom_call" | custom-call | bytes 163840 | tf_op jit(solution)/shard_map/pallas_call | solution.py:290
  (3 shorter events, 0.0 us)
Async XLA Ops:
  0.6 0.7 %copy-start = (bf16[1,4608]{1,0:T(2,128)(2,1)S(1)}, bf16[1,4608]{1,0:T(2,128)(2,1)}, u32[]{:S(2)}) copy-start(bf16[1,4608]{1,0:T(2,128)(2,1)} %ref_ref.1) | copy-start | bytes 27652
  1.4 14.1 %copy-start.1 = (f32[16]{0:T(128)S(1)}, f32[16]{0:T(128)}, u32[]{:S(2)}) copy-start(f32[16]{0:T(128)} %param.9) | copy-start | bytes 196
  2.1 13.4 %all-to-all-start = ((bf16[16,40,128]{2,1,0:T(8,128)(2,1)}), bf16[16,40,128]{2,1,0:T(8,128)(2,1)S(1)}, u32[]{:S(2)}, u32[]{:S(2)}) async-start(bf16[16,40,128]{2,1,0:T(8,128)(2,1)} %broadcast_in_dim.2), calls=%async_computation | async-start | bytes 327680 | tf_op jit(solution)/shard_map/all_to_all | solution.py:335
  15.5 1.2 %collective-permute-start.1 = (f32[1,128]{1,0:T(1,128)S(1)}, f32[1,128]{1,0:T(1,128)S(1)}, u32[]{:S(2)}, u32[]{:S(2)}) collective-permute-start(f32[1,128]{1,0:T(1,128)S(1)} %get-tuple-element.19.refs_6_), channel_id=1, source_target_pairs={{0,1},{1,0},{2,3},{3,2},{4,5},{5,4},{6,7},{7,6},{8,9},{9,8},{10,11... | collective-permute-start | bytes 1544 | tf_op jit(solution)/shard_map/ppermute | solution.py:366
  16.6 1.2 %collective-permute-start = (f32[1,128]{1,0:T(1,128)S(1)}, f32[1,128]{1,0:T(1,128)S(1)}, u32[]{:S(2)}, u32[]{:S(2)}) collective-permute-start(f32[1,128]{1,0:T(1,128)S(1)} %get-tuple-element.23.refs_4_.rest_0_), channel_id=1, source_target_pairs={{0,1},{1,0},{2,3},{3,2},{4,5},{5,4},{6,7},{7,6},{8,9},{9,8},{10,11... | collective-permute-start | bytes 1544 | tf_op jit(solution)/shard_map/ppermute | solution.py:370

commit v6 on v5

--- a/solution.py
+++ b/solution.py
@@ -16,6 +16,7 @@
 LANES = 128
 HALF = ROT // 2
 PARTS = 4
+DEPTH = 4
 AHEAD = 6
 CHUNK = 40
 ORDER = [11, 10, 0, 5, 6, 4, 14, 1, 15, 8, 13, 7, 3, 2, 12, 9]
@@ -67,14 +68,12 @@
 
 
 def retile_kernel(ref_ref, out_ref, rows):
-    owned = ref_ref.shape[0]
-    blocks = ref_ref.shape[1] // LANES
+    owned, depth, width = out_ref.shape
     for o in range(owned):
         row = ref_ref[o : o + 1, :].astype(F32)
-        for j in range(blocks):
-            rows[o * CHUNK + j : o * CHUNK + j + 1, :] = row[:, j * LANES : (j + 1) * LANES]
-        rows[o * CHUNK + blocks : (o + 1) * CHUNK, :] = jnp.zeros((CHUNK - blocks, LANES), F32)
-    out_ref[...] = rows[...].astype(BF16)
+        for a in range(depth):
+            rows[a : a + 1, :] = row[:, a * width : (a + 1) * width]
+        out_ref[o] = rows[...].astype(BF16)
 
 
 def prepare_kernel(
@@ -150,11 +149,17 @@
         place = jnp.where(row == i, c, place)
     diagonal = place == lax.broadcasted_iota(jnp.int32, (classes, classes), 1)
     prior = jnp.sum(jnp.where(diagonal, jnp.broadcast_to(prior_ref[...], (classes, classes)), 0.0), axis=1, keepdims=True)
-    wide[...] = got_ref[...].astype(F32)
+    depth, width = got_ref.shape[1:]
+    across = width // LANES
+    for i in range(classes):
+        message = got_ref[i].astype(F32)
+        for b in range(across):
+            at = (b * classes + i) * depth
+            wide[at : at + depth, :] = message[:, b * LANES : (b + 1) * LANES]
     blocks = []
     ref_power = jnp.zeros((classes, LANES), F32)
     for j in range(ROT):
-        block = wide[pl.ds(j, classes, stride=CHUNK), :]
+        block = wide[pl.ds(j % across * classes * depth + j // across, classes, stride=depth), :]
         ref_power = ref_power + block * block
         blocks.append(block.astype(BF16))
     energy = 0.5 * lax.dot_general(
@@ -325,13 +330,14 @@
         axis_index_groups=[order],
         tiled=True,
     )
+    width = samples // DEPTH
     (own,) = call(
         retile_kernel,
-        [((owned * CHUNK, LANES), BF16)],
-        [pltpu.VMEM((owned * CHUNK, LANES), F32)],
-        bytes_accessed=message * LANES * 2,
+        [((owned, DEPTH, width), BF16)],
+        [pltpu.VMEM((DEPTH, width), F32)],
+        bytes_accessed=owned * samples * 4,
     )(references)
-    spread = jnp.broadcast_to(own[None], (dom_size, owned * CHUNK, LANES)).reshape(message, LANES)
+    spread = jnp.broadcast_to(own[None], (dom_size, owned, DEPTH, width)).reshape(classes, DEPTH, width)
     got = exchange(spread)
     adjusted, turned, power = call(
         prepare_kernel,
@@ -355,16 +361,17 @@
     held = [d * owned + o for d in order for o in range(owned)]
     prior = log_prior.reshape(1, classes)
     scored = [((HALF * classes, 2 * rows), F32), ((1, rows), F32), ((1, rows), F32)]
+    spots = [pltpu.VMEM((classes * samples // LANES, LANES), F32)]
     wide = [pltpu.VMEM((message, LANES), F32)]
     costs = dict(flops=dot_flops, bytes_accessed=rows * samples * 4)
     summed = [((message, LANES), BF16)]
     two = cls_size == 2
-    e, best, lse = call(functools.partial(first_score_kernel, held, not two), scored, wide, **costs)(
+    e, best, lse = call(functools.partial(first_score_kernel, held, not two), scored, spots, **costs)(
         got, turned, power, prior
     )
     if two:
         early = lax.ppermute(lse, "cls", [(0, 1), (1, 0)])
-        e, best, lse = call(functools.partial(second_score_kernel, held), scored, wide, **costs)(
+        e, best, lse = call(functools.partial(second_score_kernel, held), scored, spots, **costs)(
             got, turned, power, prior, e, best, lse
         )
         all_lse = (lse, lax.ppermute(lse, "cls", [(0, 1), (1, 0)]))

time: 29.5 us -> 29.3 us (level)
    reshape x0 -> x1, local copies, waits for them, and re-layouts: none -> 0.69 us  [per_device(): jnp.broadcast_to(own[None], (dom_size, owned, DEPTH, width))]
    broadcast_in_dim x1 -> x0, local copies, waits for them, and re-layouts: 0.68 us -> none  [per_device(): jnp.broadcast_to(own[None], (dom_size, owned * CHUNK, LANES))]
where the time goes in v6:
time: 29.3 us; the launch traced here: 29 us
  blocking collectives  10.6 us (36%)
  starting transfers between devices  9.41 us (32%)
  Pallas kernels  6.11 us (21%)
  local copies, waits for them, and re-layouts  1.41 us (5%)
  waiting for transfers between devices  0.72 us (2%)
  between operations  0.69 us (2%)
    all_to_all x1, blocking collectives, per_device(): mine = exchange(partial_sums)  10.6 us
    all_to_all x1, starting transfers between devices, per_device(): got = exchange(spread)  9.23 us
    pallas_call x7, Pallas kernels, run(): pl.pallas_call(kernel, out_shape=tuple((jax.ShapeDtypeStruct(shape, dtype...  6.11 us
    unnamed x4, local copies, waits for them, and re-layouts  0.72 us
    reshape x1, local copies, waits for them, and re-layouts, per_device(): jnp.broadcast_to(own[None], (dom_size, owned, DEPTH, width))  0.69 us
    all_to_all x1, waiting for transfers between devices, per_device(): got = exchange(spread)  0.61 us
  transfers between devices with their start and end apart: 3, of which 2 were waited for; matrix products, arithmetic and copies ran while one was open for 0% of the time, Pallas kernels for 19%

profile of v6, /device:TPU:0, one launch (start us, length us, event | category | flops | bytes accessed | tf_op | source)
XLA Modules:
  0.0 29.0 jit_solution(2002817764401666777)
XLA Ops:
  0.6 0.0 copy-start
  0.6 0.7 %copy-done = bf16[1,4608]{1,0:T(2,128)(2,1)S(1)} copy-done((bf16[1,4608]{1,0:T(2,128)(2,1)S(1)}, bf16[1,4608]{1,0:T(2,128)(2,1)}, u32[]{:S(2)}) %copy-start) | copy-done | bytes 9240
  1.4 0.0 copy-start.1
  1.4 0.7 %reshape.26 = bf16[16,4,1152]{2,1,0:T(4,128)(2,1)} broadcast(bf16[4,1152]{1,0:T(4,128)(2,1)S(1)} %bitcast.10), dimensions={1,2} | broadcast | bytes 156672 | tf_op jit(solution)/shard_map/reshape | solution.py:340
  2.1 9.2 %all-to-all-start = ((bf16[16,4,1152]{2,1,0:T(4,128)(2,1)}), bf16[16,4,1152]{2,1,0:T(4,128)(2,1)S(1)}, u32[]{:S(2)}, u32[]{:S(2)}) async-start(bf16[16,4,1152]{2,1,0:T(4,128)(2,1)} %reshape.26), calls=%async_computation | async-start | bytes 294912 | tf_op jit(solution)/shard_map/all_to_all | solution.py:341
  11.3 3.4 %shard_map.95 = (bf16[128,4608]{1,0:T(8,128)(2,1)S(1)}, bf16[4608,128]{1,0:T(8,128)(2,1)S(1)}, f32[128,128]{1,0:T(8,128)S(1)}) custom-call(bf16[128,4608]{1,0:T(8,128)(2,1)} %x_hbm.1, s32[2,128]{1,0:T(2,128)} %bitcast.13, s32[1,128]{1,0:T(1,128)} %bitcast.14, f32[1,32]{1,0:T(1,128)} %bitcast.15, f32[40,128]{1,0:T(8,128)} %constant.2.clone.table_hbm), custom_call_target="tpu_custom_call" | custom-call | flops 176947200 | bytes 3538944 | tf_op jit(solution)/shard_map/pallas_call | solution.py:295
  14.7 0.6 %all-to-all-done.refs_0_ = bf16[16,4,1152]{2,1,0:T(4,128)(2,1)S(1)} async-done(((bf16[16,4,1152]{2,1,0:T(4,128)(2,1)}), bf16[16,4,1152]{2,1,0:T(4,128)(2,1)S(1)}, u32[]{:S(2)}, u32[]{:S(2)}) %all-to-all-start) | async-done | bytes 147488 | tf_op jit(solution)/shard_map/all_to_all | solution.py:341
  15.3 0.0 copy-done.1
  15.3 0.1 collective-permute-start.1
  15.4 1.1 %shard_map.97 = (f32[288,256]{1,0:T(8,128)S(1)}, f32[1,128]{1,0:T(1,128)S(1)}, f32[1,128]{1,0:T(1,128)S(1)}) custom-call(bf16[16,4,1152]{2,1,0:T(4,128)(2,1)S(1)} %all-to-all-done.refs_0_, bf16[4608,128]{1,0:T(8,128)(2,1)S(1)} %get-tuple-element.15.refs_1_, f32[128,128]{1,0:T(8,128)S(1)} %get-tuple-element.16.refs_2_.refs_3_, f32[1,16]{1,0:T(1,128)S(1)} %bitcast.12, ...), custom_call_target="tpu_custom_call" | custom-call | flops 679477248 | bytes 2359296 | tf_op jit(solution)/shard_map/pallas_call | solution.py:295
  16.5 0.1 collective-permute-start
  16.6 0.0 collective-permute-done.1.refs_5_
  16.6 1.0 %shard_map.98.refs_6_ = bf16[640,128]{1,0:T(8,128)(2,1)S(1)} custom-call(f32[288,256]{1,0:T(8,128)S(1)} %get-tuple-element.20.refs_0_, f32[1,128]{1,0:T(1,128)S(1)} %get-tuple-element.21.refs_1_, bf16[128,4608]{1,0:T(8,128)(2,1)S(1)} %get-tuple-element.22.refs_2_, f32[128,128]{1,0:T(8,128)S(1)} %get-tuple-element.16.refs_2_.refs_3_, ...), custom_call_target="tpu_custom_call" | custom-call | flops 679477248 | bytes 2359296 | tf_op jit(solution)/shard_map/pallas_call | solution.py:295
  17.6 0.1 collective-permute-done.refs_5_.rest_1_
  17.7 10.6 %all_to_all.16 = bf16[16,40,128]{2,1,0:T(8,128)(2,1)S(1)} all-to-all(bf16[16,40,128]{2,1,0:T(8,128)(2,1)S(1)} %bitcast.9), channel_id=1, replica_groups={{22,20,0,10,12,8,28,2,30,16,26,14,6,4,24,18},{23,21,1,11,13,9,29,3,31,1..., dimensions={0} | all-to-all | bytes 327680 | tf_op jit(solution)/shard_map/all_to_all | solution.py:387
  28.3 0.6 %shard_map.100 = (f32[1,4608]{1,0:T(1,128)}, f32[1,32]{1,0:T(1,128)}, f32[1,128]{1,0:T(1,128)}) custom-call(bf16[640,128]{1,0:T(8,128)(2,1)S(1)} %bitcast.8, f32[1,128]{1,0:T(1,128)S(1)} %get-tuple-element.23.refs_4_.rest_0_, f32[1,128]{1,0:T(1,128)S(1)} %collective-permute-done.refs_5_.rest_1_), custom_call_target="tpu_custom_call" | custom-call | bytes 163840 | tf_op jit(solution)/shard_map/pallas_call | solution.py:295
  (3 shorter events, 0.0 us)
Async XLA Ops:
  0.6 0.7 %copy-start = (bf16[1,4608]{1,0:T(2,128)(2,1)S(1)}, bf16[1,4608]{1,0:T(2,128)(2,1)}, u32[]{:S(2)}) copy-start(bf16[1,4608]{1,0:T(2,128)(2,1)} %ref_ref.1) | copy-start | bytes 27652
  1.4 13.9 %copy-start.1 = (f32[16]{0:T(128)S(1)}, f32[16]{0:T(128)}, u32[]{:S(2)}) copy-start(f32[16]{0:T(128)} %param.9) | copy-start | bytes 196
  2.1 13.2 %all-to-all-start = ((bf16[16,4,1152]{2,1,0:T(4,128)(2,1)}), bf16[16,4,1152]{2,1,0:T(4,128)(2,1)S(1)}, u32[]{:S(2)}, u32[]{:S(2)}) async-start(bf16[16,4,1152]{2,1,0:T(4,128)(2,1)} %reshape.26), calls=%async_computation | async-start | bytes 294912 | tf_op jit(solution)/shard_map/all_to_all | solution.py:341
  15.3 1.3 %collective-permute-start.1 = (f32[1,128]{1,0:T(1,128)S(1)}, f32[1,128]{1,0:T(1,128)S(1)}, u32[]{:S(2)}, u32[]{:S(2)}) collective-permute-start(f32[1,128]{1,0:T(1,128)S(1)} %get-tuple-element.19.refs_6_), channel_id=1, source_target_pairs={{0,1},{1,0},{2,3},{3,2},{4,5},{5,4},{6,7},{7,6},{8,9},{9,8},{10,11... | collective-permute-start | bytes 1544 | tf_op jit(solution)/shard_map/ppermute | solution.py:373
  16.5 1.2 %collective-permute-start = (f32[1,128]{1,0:T(1,128)S(1)}, f32[1,128]{1,0:T(1,128)S(1)}, u32[]{:S(2)}, u32[]{:S(2)}) collective-permute-start(f32[1,128]{1,0:T(1,128)S(1)} %get-tuple-element.23.refs_4_.rest_0_), channel_id=1, source_target_pairs={{0,1},{1,0},{2,3},{3,2},{4,5},{5,4},{6,7},{7,6},{8,9},{9,8},{10,11... | collective-permute-start | bytes 1544 | tf_op jit(solution)/shard_map/ppermute | solution.py:377

commit v7 on v6

--- a/solution.py
+++ b/solution.py
@@ -18,7 +18,7 @@
 PARTS = 4
 DEPTH = 4
 AHEAD = 6
-CHUNK = 40
+ACROSS = 19
 ORDER = [11, 10, 0, 5, 6, 4, 14, 1, 15, 8, 13, 7, 3, 2, 12, 9]
 F32 = jnp.float32
 BF16 = jnp.bfloat16
@@ -218,6 +218,10 @@
     return top + jnp.log(jnp.sum(jnp.exp(lse - top), axis=0, keepdims=True))
 
 
+def spot(n, classes):
+    return pl.ds(n % ACROSS * classes * 2 + n // ACROSS, classes, stride=2)
+
+
 def sums(e_ref, best_ref, adj_ref, power_ref, *rest):
     *lse_refs, out_ref, wide = rest
     particles = adj_ref.shape[0]
@@ -242,16 +246,19 @@
     data = jnp.dot(lhs, rhs, preferred_element_type=F32)
     for n in range(ROT):
         r, d = n // 2, n % 2
-        wide[pl.ds(n, classes, stride=CHUNK), :] = data[r * classes : (r + 1) * classes, d * LANES : (d + 1) * LANES]
+        wide[spot(n, classes), :] = data[r * classes : (r + 1) * classes, d * LANES : (d + 1) * LANES]
     group = lax.broadcasted_iota(jnp.int32, weight.shape, 1) // CYCLES
     high = weight.astype(BF16).astype(F32)
     rest = weight - high
     middle = rest.astype(BF16).astype(F32)
     terms = jnp.where(group == 0, high, jnp.where(group == 1, middle, jnp.where(group == 2, rest - middle, 0.0)))
-    wide[pl.ds(ROT, classes, stride=CHUNK), :] = terms
-    for n in range(ROT + 1, CHUNK):
-        wide[pl.ds(n, classes, stride=CHUNK), :] = jnp.zeros((classes, LANES), F32)
-    out_ref[...] = wide[...].astype(BF16)
+    wide[spot(ROT, classes), :] = terms
+    for n in range(ROT + 1, 2 * ACROSS):
+        wide[spot(n, classes), :] = jnp.zeros((classes, LANES), F32)
+    for c in range(classes):
+        out_ref[c] = jnp.concatenate(
+            [wide[(b * classes + c) * 2 : (b * classes + c + 1) * 2, :] for b in range(ACROSS)], axis=1
+        ).astype(BF16)
 
 
 def first_sum_kernel(alone, *refs):
@@ -277,13 +284,16 @@
     *lse_refs, data_ref, weight_ref, evidence_ref = rest
     evidence_ref[...] = total_evidence(lse_refs)
     owned = data_ref.shape[0]
-    got = got_ref[...].astype(F32).reshape(senders, owned * CHUNK, LANES)
-    total = jnp.sum(got, axis=0)
     for o in range(owned):
-        base = o * CHUNK
+        total = got_ref[o].astype(F32)
+        for k in range(1, senders):
+            total = total + got_ref[k * owned + o].astype(F32)
+        blocks = [
+            total[n // ACROSS : n // ACROSS + 1, n % ACROSS * LANES : (n % ACROSS + 1) * LANES] for n in range(ROT + 1)
+        ]
         for n in range(ROT):
-            data_ref[o : o + 1, n * LANES : (n + 1) * LANES] = total[base + n : base + n + 1, :]
-        terms = total[base + ROT : base + ROT + 1, :]
+            data_ref[o : o + 1, n * LANES : (n + 1) * LANES] = blocks[n]
+        terms = blocks[ROT]
         weight_ref[o : o + 1, :] = (
             terms[:, :CYCLES] + terms[:, CYCLES : 2 * CYCLES] + terms[:, 2 * CYCLES : 3 * CYCLES]
         )
@@ -318,7 +328,7 @@
     rows, samples = particles.shape
     owned = references.shape[0]
     classes = log_prior.shape[0]
-    message = classes * CHUNK
+    message = classes * 2 * ACROSS
     table = lane_tables()
 
     order = exchange_order(dom_size)
@@ -364,7 +374,7 @@
     spots = [pltpu.VMEM((classes * samples // LANES, LANES), F32)]
     wide = [pltpu.VMEM((message, LANES), F32)]
     costs = dict(flops=dot_flops, bytes_accessed=rows * samples * 4)
-    summed = [((message, LANES), BF16)]
+    summed = [((classes, 2, ACROSS * LANES), BF16)]
     two = cls_size == 2
     e, best, lse = call(functools.partial(first_score_kernel, held, not two), scored, spots, **costs)(
         got, turned, power, prior

time: 29.3 us -> 29.2 us (level)
  no operation moved by 1% of the time
where the time goes in v7:
time: 29.2 us; the launch traced here: 28.9 us
  blocking collectives  10.5 us (36%)
  starting transfers between devices  9.41 us (32%)
  Pallas kernels  6.17 us (21%)
  local copies, waits for them, and re-layouts  1.41 us (5%)
  between operations  0.69 us (2%)
  waiting for transfers between devices  0.67 us (2%)
    all_to_all x1, blocking collectives, per_device(): mine = exchange(partial_sums)  10.5 us
    all_to_all x1, starting transfers between devices, per_device(): got = exchange(spread)  9.23 us
    pallas_call x7, Pallas kernels, run(): pl.pallas_call(kernel, out_shape=tuple((jax.ShapeDtypeStruct(shape, dtype...  6.17 us
    unnamed x4, local copies, waits for them, and re-layouts  0.72 us
    reshape x1, local copies, waits for them, and re-layouts, per_device(): jnp.broadcast_to(own[None], (dom_size, owned, DEPTH, width))  0.69 us
    all_to_all x1, waiting for transfers between devices, per_device(): got = exchange(spread)  0.61 us
  transfers between devices with their start and end apart: 3, of which 2 were waited for; matrix products, arithmetic and copies ran while one was open for 0% of the time, Pallas kernels for 19%

profile of v7, /device:TPU:0, one launch (start us, length us, event | category | flops | bytes accessed | tf_op | source)
XLA Modules:
  0.0 28.9 jit_solution(5580196623913771946)
XLA Ops:
  0.6 0.0 copy-start
  0.6 0.7 %copy-done = bf16[1,4608]{1,0:T(2,128)(2,1)S(1)} copy-done((bf16[1,4608]{1,0:T(2,128)(2,1)S(1)}, bf16[1,4608]{1,0:T(2,128)(2,1)}, u32[]{:S(2)}) %copy-start) | copy-done | bytes 9240
  1.4 0.0 copy-start.1
  1.4 0.7 %reshape.24 = bf16[16,4,1152]{2,1,0:T(4,128)(2,1)} broadcast(bf16[4,1152]{1,0:T(4,128)(2,1)S(1)} %bitcast.6), dimensions={1,2} | broadcast | bytes 156672 | tf_op jit(solution)/shard_map/reshape | solution.py:350
  2.1 9.2 %all-to-all-start = ((bf16[16,4,1152]{2,1,0:T(4,128)(2,1)}), bf16[16,4,1152]{2,1,0:T(4,128)(2,1)S(1)}, u32[]{:S(2)}, u32[]{:S(2)}) async-start(bf16[16,4,1152]{2,1,0:T(4,128)(2,1)} %reshape.24), calls=%async_computation | async-start | bytes 294912 | tf_op jit(solution)/shard_map/all_to_all | solution.py:351
  11.3 3.4 %shard_map.95 = (bf16[128,4608]{1,0:T(8,128)(2,1)S(1)}, bf16[4608,128]{1,0:T(8,128)(2,1)S(1)}, f32[128,128]{1,0:T(8,128)S(1)}) custom-call(bf16[128,4608]{1,0:T(8,128)(2,1)} %x_hbm.1, s32[2,128]{1,0:T(2,128)} %bitcast.9, s32[1,128]{1,0:T(1,128)} %bitcast.10, f32[1,32]{1,0:T(1,128)} %bitcast.11, f32[40,128]{1,0:T(8,128)} %constant.2.clone.table_hbm), custom_call_target="tpu_custom_call" | custom-call | flops 176947200 | bytes 3538944 | tf_op jit(solution)/shard_map/pallas_call | solution.py:305
  14.7 0.6 %all-to-all-done.refs_0_ = bf16[16,4,1152]{2,1,0:T(4,128)(2,1)S(1)} async-done(((bf16[16,4,1152]{2,1,0:T(4,128)(2,1)}), bf16[16,4,1152]{2,1,0:T(4,128)(2,1)S(1)}, u32[]{:S(2)}, u32[]{:S(2)}) %all-to-all-start) | async-done | bytes 147488 | tf_op jit(solution)/shard_map/all_to_all | solution.py:351
  15.3 0.0 copy-done.1
  15.3 0.1 collective-permute-start.1
  15.4 1.1 %shard_map.97 = (f32[288,256]{1,0:T(8,128)S(1)}, f32[1,128]{1,0:T(1,128)S(1)}, f32[1,128]{1,0:T(1,128)S(1)}) custom-call(bf16[16,4,1152]{2,1,0:T(4,128)(2,1)S(1)} %all-to-all-done.refs_0_, bf16[4608,128]{1,0:T(8,128)(2,1)S(1)} %get-tuple-element.15.refs_1_, f32[128,128]{1,0:T(8,128)S(1)} %get-tuple-element.16.refs_2_.refs_3_, f32[1,16]{1,0:T(1,128)S(1)} %bitcast.8, ...), custom_call_target="tpu_custom_call" | custom-call | flops 679477248 | bytes 2359296 | tf_op jit(solution)/shard_map/pallas_call | solution.py:305
  16.5 0.1 collective-permute-start
  16.6 0.0 collective-permute-done.1.refs_5_
  16.6 1.0 %shard_map.98.refs_6_ = bf16[16,2,2432]{2,1,0:T(2,128)(2,1)S(1)} custom-call(f32[288,256]{1,0:T(8,128)S(1)} %get-tuple-element.20.refs_0_, f32[1,128]{1,0:T(1,128)S(1)} %get-tuple-element.21.refs_1_, bf16[128,4608]{1,0:T(8,128)(2,1)S(1)} %get-tuple-element.22.refs_2_, f32[128,128]{1,0:T(8,128)S(1)} %get-tuple-element.16.refs_2_.refs_3_, ...), custom_call_target="tpu_custom_call" | custom-call | flops 679477248 | bytes 2359296 | tf_op jit(solution)/shard_map/pallas_call | solution.py:305
  17.6 0.1 collective-permute-done.refs_5_.rest_1_
  17.7 10.5 %all_to_all.10.got_ref = bf16[16,2,2432]{2,1,0:T(2,128)(2,1)S(1)} all-to-all(bf16[16,2,2432]{2,1,0:T(2,128)(2,1)S(1)} %shard_map.99), channel_id=1, replica_groups={{22,20,0,10,12,8,28,2,30,16,26,14,6,4,24,18},{23,21,1,11,13,9,29,3,31,1..., dimensions={0} | all-to-all | bytes 311296 | tf_op jit(solution)/shard_map/all_to_all | solution.py:397
  28.2 0.6 %shard_map.100 = (f32[1,4608]{1,0:T(1,128)}, f32[1,32]{1,0:T(1,128)}, f32[1,128]{1,0:T(1,128)}) custom-call(bf16[16,2,2432]{2,1,0:T(2,128)(2,1)S(1)} %all_to_all.10.got_ref, f32[1,128]{1,0:T(1,128)S(1)} %get-tuple-element.23.refs_4_.rest_0_, f32[1,128]{1,0:T(1,128)S(1)} %collective-permute-done.refs_5_.rest_1_), custom_call_target="tpu_custom_call" | custom-call | bytes 155648 | tf_op jit(solution)/shard_map/pallas_call | solution.py:305
  (3 shorter events, 0.0 us)
Async XLA Ops:
  0.6 0.7 %copy-start = (bf16[1,4608]{1,0:T(2,128)(2,1)S(1)}, bf16[1,4608]{1,0:T(2,128)(2,1)}, u32[]{:S(2)}) copy-start(bf16[1,4608]{1,0:T(2,128)(2,1)} %ref_ref.1) | copy-start | bytes 27652
  1.4 13.9 %copy-start.1 = (f32[16]{0:T(128)S(1)}, f32[16]{0:T(128)}, u32[]{:S(2)}) copy-start(f32[16]{0:T(128)} %param.9) | copy-start | bytes 196
  2.1 13.2 %all-to-all-start = ((bf16[16,4,1152]{2,1,0:T(4,128)(2,1)}), bf16[16,4,1152]{2,1,0:T(4,128)(2,1)S(1)}, u32[]{:S(2)}, u32[]{:S(2)}) async-start(bf16[16,4,1152]{2,1,0:T(4,128)(2,1)} %reshape.24), calls=%async_computation | async-start | bytes 294912 | tf_op jit(solution)/shard_map/all_to_all | solution.py:351
  15.3 1.3 %collective-permute-start.1 = (f32[1,128]{1,0:T(1,128)S(1)}, f32[1,128]{1,0:T(1,128)S(1)}, u32[]{:S(2)}, u32[]{:S(2)}) collective-permute-start(f32[1,128]{1,0:T(1,128)S(1)} %get-tuple-element.19.refs_6_), channel_id=1, source_target_pairs={{0,1},{1,0},{2,3},{3,2},{4,5},{5,4},{6,7},{7,6},{8,9},{9,8},{10,11... | collective-permute-start | bytes 1544 | tf_op jit(solution)/shard_map/ppermute | solution.py:383
  16.5 1.2 %collective-permute-start = (f32[1,128]{1,0:T(1,128)S(1)}, f32[1,128]{1,0:T(1,128)S(1)}, u32[]{:S(2)}, u32[]{:S(2)}) collective-permute-start(f32[1,128]{1,0:T(1,128)S(1)} %get-tuple-element.23.refs_4_.rest_0_), channel_id=1, source_target_pairs={{0,1},{1,0},{2,3},{3,2},{4,5},{5,4},{6,7},{7,6},{8,9},{9,8},{10,11... | collective-permute-start | bytes 1544 | tf_op jit(solution)/shard_map/ppermute | solution.py:387
